TPU v7x, 32 devices: a whole 2x2x4 slice. The times are simulated.
32 devices in a mesh: dp: 4 (over y, x), expert: 8 (over z, core).
Axes of the slice: x: 2, y: 2, z: 4, core: 2. Of those that a mesh axis runs over, the one named last changes fastest.
Arguments:
- tokens: bfloat16 [4096, 3584], P(('dp', 'expert')), may hold values from -6 to 6
- grad_out: bfloat16 [4096, 3584], P(('dp', 'expert')), may hold values from -1.5 to 1.5
- route: int32 [4, 8, 8, 1], P('dp', 'expert'), may hold values from 0 to 127
- gates: bfloat16 [4, 8, 8, 1], P('dp', 'expert'), may hold values from 0.099609375 to 1
- w_gate: bfloat16 [8, 3584, 768], P('expert', 'dp'), may hold values from -0.09375 to 0.09375
- w_up: bfloat16 [8, 3584, 768], P('expert', 'dp'), may hold values from -0.09375 to 0.09375
- w_down: bfloat16 [8, 768, 3584], P('expert', None, 'dp'), may hold values from -0.21875 to 0.21875
Outputs:
- grad_tokens: bfloat16 [4096, 3584], P(('dp', 'expert'))
- grad_w_gate: bfloat16 [8, 3584, 768], P('expert', 'dp')
- grad_w_up: bfloat16 [8, 3584, 768], P('expert', 'dp')
- grad_w_down: bfloat16 [8, 768, 3584], P('expert', None, 'dp')
- grad_gates: float32 [4, 8, 8, 1], P('dp', 'expert')
Inputs may be any that keep to these rules, and one draw needn't show every extreme that they name: route[i, j, e, s] is the position, among the 128 tokens of the device at dp index i and expert index j, of the token that expert e takes in slot s from that device; a token may be taken by several experts or slots.
All inputs are finite; a program needn't handle non-finite values.
Results may differ from a plain program's by a relative error of at most 0.017.
Values may be sent and summed in bfloat16 or wider, within the bound.
No kernel may reach another device: no remote copies, remote signals or barrier semaphores. Data moves between devices by JAX's collectives and lax.ppermute only.
A program may use at most 64 MiB of HBM per device.

v0:
```python
import jax
import jax.numpy as jnp
from jax import lax
from jax.sharding import PartitionSpec as P


def contract_last(left, right):
    return lax.dot_general(
        left, right, (((1,), (1,)), ((), ())), preferred_element_type=jnp.float32
    )


def contract_first(left, right):
    return lax.dot_general(
        left, right, (((0,), (0,)), ((), ())), preferred_element_type=jnp.float32
    )


def local(tokens, grad_out, route, gates, w_gate, w_up, w_down):
    n_dp = lax.axis_size("dp")
    n_ex = lax.axis_size("expert")
    experts = route.shape[2]
    slots = route.shape[3]
    width = tokens.shape[1]
    piece = width // n_dp
    capacity = n_ex * slots
    rows = n_dp * capacity
    wg = w_gate[0]
    wu = w_up[0]
    wd = w_down[0]
    own_start = lax.axis_index("dp") * capacity
    picks = route.reshape(experts * slots)
    picked_x = jnp.take(tokens, picks, axis=0).reshape(experts, 1, slots, width)
    picked_dy = jnp.take(grad_out, picks, axis=0).reshape(experts, 1, slots, width)
    gate_cols = jnp.broadcast_to(gates.reshape(experts, 1, slots, 1), (experts, 1, slots, n_dp))
    x_in = lax.all_to_all(
        lax.all_to_all(picked_x, "dp", split_axis=3, concat_axis=1, tiled=True),
        "expert",
        split_axis=0,
        concat_axis=2,
        tiled=True,
    )
    x_rows = x_in.reshape(rows, piece)
    gate_pre, up_pre = lax.psum(
        (
            jnp.dot(x_rows, wg, preferred_element_type=jnp.float32),
            jnp.dot(x_rows, wu, preferred_element_type=jnp.float32),
        ),
        "dp",
    )
    hidden_all = (jax.nn.silu(gate_pre) * up_pre).astype(jnp.bfloat16)
    out_rows = jnp.dot(hidden_all, wd, preferred_element_type=jnp.float32).astype(jnp.bfloat16)
    dy_in, g_in = (
        lax.all_to_all(
            lax.all_to_all(picked_dy, "dp", split_axis=3, concat_axis=1, tiled=True),
            "expert",
            split_axis=0,
            concat_axis=2,
            tiled=True,
        ),
        lax.all_to_all(
            lax.all_to_all(gate_cols, "dp", split_axis=3, concat_axis=1, tiled=True),
            "expert",
            split_axis=0,
            concat_axis=2,
            tiled=True,
        ),
    )
    dy_rows = dy_in.reshape(rows, piece)
    gate_rows = g_in.reshape(rows, 1)
    weighted = (gate_rows.astype(jnp.float32) * dy_rows.astype(jnp.float32)).astype(jnp.bfloat16)
    returned = lax.all_to_all(
        lax.all_to_all(
            out_rows.reshape(1, n_dp, capacity, piece),
            "dp",
            split_axis=1,
            concat_axis=3,
            tiled=True,
        ),
        "expert",
        split_axis=2,
        concat_axis=0,
        tiled=True,
    )
    grad_gates = jnp.sum(
        picked_dy.astype(jnp.float32) * returned.astype(jnp.float32), axis=3
    ).reshape(gates.shape)
    grad_own = lax.psum_scatter(contract_last(weighted, wd), "dp", scatter_dimension=0, tiled=True)
    gate_own = lax.dynamic_slice_in_dim(gate_pre, own_start, capacity, 0)
    up_own = lax.dynamic_slice_in_dim(up_pre, own_start, capacity, 0)
    sig = jax.nn.sigmoid(gate_own)
    gate_share = (grad_own * up_own * sig * (1.0 + gate_own * (1.0 - sig))).astype(jnp.bfloat16)
    up_share = (grad_own * gate_own * sig).astype(jnp.bfloat16)
    grad_gate_pre, grad_up_pre = (
        lax.all_gather(gate_share, "dp", axis=0, tiled=True),
        lax.all_gather(up_share, "dp", axis=0, tiled=True),
    )
    grad_rows = (contract_last(grad_gate_pre, wg) + contract_last(grad_up_pre, wu)).astype(
        jnp.bfloat16
    )
    grad_wg = contract_first(x_rows, grad_gate_pre).astype(jnp.bfloat16)[None]
    grad_wu = contract_first(x_rows, grad_up_pre).astype(jnp.bfloat16)[None]
    grad_wd = contract_first(hidden_all, weighted).astype(jnp.bfloat16)[None]
    back = lax.all_to_all(
        lax.all_to_all(
            grad_rows.reshape(1, n_dp, capacity, piece),
            "dp",
            split_axis=1,
            concat_axis=3,
            tiled=True,
        ),
        "expert",
        split_axis=2,
        concat_axis=0,
        tiled=True,
    )
    flat = back.reshape(experts * slots, width).astype(jnp.float32)
    grad_tokens = (
        jnp.zeros((tokens.shape[0], width), jnp.float32).at[picks].add(flat).astype(jnp.bfloat16)
    )
    return (grad_tokens, grad_wg, grad_wu, grad_wd, grad_gates)


def solution(mesh):
    return jax.shard_map(
        local,
        mesh=mesh,
        in_specs=(
            P(("dp", "expert"), None),
            P(("dp", "expert"), None),
            P("dp", "expert", None, None),
            P("dp", "expert", None, None),
            P("expert", "dp", None),
            P("expert", "dp", None),
            P("expert", None, "dp"),
        ),
        out_specs=(
            P(("dp", "expert"), None),
            P("expert", "dp", None),
            P("expert", "dp", None),
            P("expert", None, "dp"),
            P("dp", "expert", None, None),
        ),
        check_vma=False,
    )
```

profile of v0, /device:TPU:0, one launch (start us, length us, event | category | flops | bytes accessed | tf_op | source)
XLA Modules:
  0.0 218.6 jit_solution(12358638342042095072)
XLA Ops:
  8.5 5.2 %all-to-all-start = ((bf16[8,1,1,4]{0,2,1,3:T(2,128)(2,1)}), bf16[8,1,1,4]{0,2,1,3:T(2,128)(2,1)S(1)}, u32[]{:S(2)}, u32[]{:S(2)}) async-start(bf16[8,1,1,4]{0,2,1,3:T(2,128)(2,1)} %broadcast_in_dim.31), calls=%async_computation | async-start | bytes 4096 | tf_op jit(solution)/shard_map/all_to_all | solution.py:62
  19.0 2.5 %copy.43 = bf16[8,1,1,3584]{0,2,1,3:T(2,128)(2,1)S(1)} copy(bf16[8,1,1,3584]{3,0,2,1:T(8,128)(2,1)S(1)} %get-tuple-element.14) | data formatting | bytes 114688 | tf_op jit(solution)/shard_map/reshape | solution.py:33
  22.2 4.9 %all-to-all-start.1 = ((bf16[8,4,1,1]{1,3,2,0:T(2,128)(2,1)}), bf16[8,4,1,1]{1,3,2,0:T(2,128)(2,1)S(1)}, u32[]{:S(2)}, u32[]{:S(2)}) async-start(bf16[8,4,1,1]{1,3,2,0:T(2,128)(2,1)} %copy.37), calls=%async_computation.1 | async-start | bytes 8192 | tf_op jit(solution)/shard_map/all_to_all | solution.py:61
  27.6 20.6 %reduce.2 = bf16[3584,8]{1,0:T(8,128)(2,1)} reduce(bf16[3584,1,1,8]{3,2,1,0:T(2,128)(2,1)S(1)} %bitcast.156, bf16[]{:T(256)} %broadcast.72), dimensions={1,2}, to_apply=%bitcast.136.reduce_sub_computation | reduce | bytes 114690
  48.2 2.7 %reshape.182 = bf16[4,2,3584]{2,1,0:T(2,128)(2,1)} reshape(bf16[3584,8]{1,0:T(8,128)(2,1)} %reduce.2) | data formatting | bytes 114688
  50.9 4.2 %all-to-all-start.4 = ((bf16[4,2,3584]{2,1,0:T(2,128)(2,1)}), bf16[4,2,3584]{2,1,0:T(2,128)(2,1)S(1)}, u32[]{:S(2)}, u32[]{:S(2)}) async-start(bf16[4,2,3584]{2,1,0:T(2,128)(2,1)} %reshape.182), calls=%async_computation.4 | async-start | bytes 114688 | tf_op jit(solution)/shard_map/all_to_all | solution.py:37
  55.1 2.4 %copy.39 = bf16[8,1,1,3584]{0,2,1,3:T(2,128)(2,1)S(1)} copy(bf16[8,1,1,3584]{3,0,2,1:T(8,128)(2,1)S(1)} %get-tuple-element.13) | data formatting | bytes 114688 | tf_op jit(solution)/shard_map/reshape | solution.py:34
  57.5 20.6 %reduce.3 = bf16[3584,8]{1,0:T(8,128)(2,1)} reduce(bf16[3584,1,1,8]{3,2,1,0:T(2,128)(2,1)S(1)} %bitcast.157, bf16[]{:T(256)} %broadcast.72), dimensions={1,2}, to_apply=%bitcast.138.reduce_sub_computation | reduce | bytes 114690
  78.1 2.7 %reshape.184 = bf16[4,2,3584]{2,1,0:T(2,128)(2,1)} reshape(bf16[3584,8]{1,0:T(8,128)(2,1)} %reduce.3) | data formatting | bytes 114688
  80.9 4.2 %all-to-all-start.2 = ((bf16[4,2,3584]{2,1,0:T(2,128)(2,1)}), bf16[4,2,3584]{2,1,0:T(2,128)(2,1)S(1)}, u32[]{:S(2)}, u32[]{:S(2)}) async-start(bf16[4,2,3584]{2,1,0:T(2,128)(2,1)} %reshape.184), calls=%async_computation.2 | async-start | bytes 114688 | tf_op jit(solution)/shard_map/all_to_all | solution.py:55
  89.9 5.1 %all-to-all-start.5 = ((bf16[8,4,1,896]{3,1,2,0:T(4,128)(2,1)}), bf16[8,4,1,896]{3,1,2,0:T(4,128)(2,1)S(1)}, u32[]{:S(2)}, u32[]{:S(2)}) async-start(bf16[8,4,1,896]{3,1,2,0:T(4,128)(2,1)} %bitcast.14), calls=%async_computation.5 | async-start | bytes 114688 | tf_op jit(solution)/shard_map/all_to_all | solution.py:36
  100.9 3.9 %all-to-all-start.3 = ((bf16[8,4,1,896]{3,1,2,0:T(4,128)(2,1)}), bf16[8,4,1,896]{3,1,2,0:T(4,128)(2,1)S(1)}, u32[]{:S(2)}, u32[]{:S(2)}) async-start(bf16[8,4,1,896]{3,1,2,0:T(4,128)(2,1)} %bitcast.8), calls=%async_computation.3 | async-start | bytes 114688 | tf_op jit(solution)/shard_map/all_to_all | solution.py:54
  106.7 3.9 %all-to-all-done.3 = bf16[8,4,1,896]{3,1,2,0:T(4,128)(2,1)S(1)} async-done(((bf16[8,4,1,896]{3,1,2,0:T(4,128)(2,1)}), bf16[8,4,1,896]{3,1,2,0:T(4,128)(2,1)S(1)}, u32[]{:S(2)}, u32[]{:S(2)}) %all-to-all-start.3) | async-done | bytes 57376 | tf_op jit(solution)/shard_map/all_to_all | solution.py:54
  110.6 2.5 %fusion.13 = f32[32,768]{1,0:T(8,128)} fusion(bf16[1,768,896]{2,1,0:T(8,128)(2,1)} %param.15, f32[4,8]{1,0:T(4,128)S(1)} %get-tuple-element.12, bf16[8,4,1,896]{3,1,2,0:T(4,128)(2,1)S(1)} %all-to-all-done.3), kind=kOutput, calls=%fused_computation.19 | convolution fusion | flops 44126208 | bytes 1532032 | tf_op jit(solution)/shard_map/dot_general | solution.py:8
  114.5 41.6 %all-reduce.4.cloned.1.call-done = (f32[32,768]{1,0:T(8,128)}, f32[32,768]{1,0:T(8,128)}, f32[32,768]{1,0:T(8,128)}) async-done(((f32[32,768]{1,0:T(8,128)}, f32[32,768]{1,0:T(8,128)}, f32[32,768]{1,0:T(8,128)}), (f32[32,768]{1,0:T(8,128)}, f32[32,768]{1,0:T(8,128)}, f32[32,768]{1,0:T(8,128)})) %all-reduce.4.cloned.1.call-update) | async-done | bytes 294928 | tf_op jit(solution)/shard_map/psum | solution.py:44
  157.9 8.2 %all_gather.6 = bf16[32,768]{1,0:T(8,128)(2,1)S(1)} all-gather(bf16[8,768]{1,0:T(8,128)(2,1)S(1)} %get-tuple-element.10), channel_id=1, replica_groups=mesh['dp'=4,'expert'=8] {'dp'}, dimensions={0}, use_global_device_ids=true | all-gather | bytes 61440 | tf_op jit(solution)/shard_map/all_gather | solution.py:95
  166.6 7.3 %all_gather.7 = bf16[32,768]{1,0:T(8,128)(2,1)S(1)} all-gather(bf16[8,768]{1,0:T(8,128)(2,1)S(1)} %get-tuple-element.9), channel_id=1, replica_groups=mesh['dp'=4,'expert'=8] {'dp'}, dimensions={0}, use_global_device_ids=true | all-gather | bytes 61440 | tf_op jit(solution)/shard_map/all_gather | solution.py:96
  175.1 3.3 %all-to-all-start.6 = ((bf16[1,4,8,896]{3,2,0,1:T(8,128)(2,1)}), bf16[1,4,8,896]{3,2,0,1:T(8,128)(2,1)S(1)}, u32[]{:S(2)}, u32[]{:S(2)}) async-start(bf16[1,4,8,896]{3,2,0,1:T(8,128)(2,1)} %fusion.27), calls=%async_computation.6 | async-start | bytes 114688 | tf_op jit(solution)/shard_map/all_to_all | solution.py:105
  178.4 2.3 %fusion.24 = bf16[1,4,8,896]{3,2,0,1:T(8,128)(2,1)} fusion(bf16[32,768]{1,0:T(8,128)(2,1)S(1)} %multiply_convert_fusion, bf16[1,768,896]{2,1,0:T(8,128)(2,1)} %param.15), kind=kOutput, calls=%fused_computation.24 | convolution fusion | flops 44068864 | bytes 1482752 | tf_op jit(solution)/shard_map/dot_general | solution.py:52
  183.2 3.3 %all-to-all-start.8 = ((bf16[1,4,8,896]{3,2,0,1:T(8,128)(2,1)}), bf16[1,4,8,896]{3,2,0,1:T(8,128)(2,1)S(1)}, u32[]{:S(2)}, u32[]{:S(2)}) async-start(bf16[1,4,8,896]{3,2,0,1:T(8,128)(2,1)} %fusion.24), calls=%async_computation.8 | async-start | bytes 114688 | tf_op jit(solution)/shard_map/all_to_all | solution.py:73
  191.3 4.6 %all-to-all-start.7 = ((bf16[8,2,1792]{2,1,0:T(2,128)(2,1)}), bf16[8,2,1792]{2,1,0:T(2,128)(2,1)S(1)}, u32[]{:S(2)}, u32[]{:S(2)}) async-start(bf16[8,2,1792]{2,1,0:T(2,128)(2,1)} %reshape.186), calls=%async_computation.7 | async-start | bytes 114688 | tf_op jit(solution)/shard_map/all_to_all | solution.py:104
  199.3 2.5 %all-to-all-done.7 = bf16[8,2,1792]{2,1,0:T(2,128)(2,1)S(1)} async-done(((bf16[8,2,1792]{2,1,0:T(2,128)(2,1)}), bf16[8,2,1792]{2,1,0:T(2,128)(2,1)S(1)}, u32[]{:S(2)}, u32[]{:S(2)}) %all-to-all-start.7) | async-done | bytes 57376 | tf_op jit(solution)/shard_map/all_to_all | solution.py:104
  201.8 3.3 %all-to-all-start.9 = ((bf16[8,2,1792]{2,1,0:T(2,128)(2,1)}), bf16[8,2,1792]{2,1,0:T(2,128)(2,1)S(1)}, u32[]{:S(2)}, u32[]{:S(2)}) async-start(bf16[8,2,1792]{2,1,0:T(2,128)(2,1)} %reshape.188), calls=%async_computation.9 | async-start | bytes 114688 | tf_op jit(solution)/shard_map/all_to_all | solution.py:72
  207.6 3.4 %all-to-all-done.9 = bf16[8,2,1792]{2,1,0:T(2,128)(2,1)S(1)} async-done(((bf16[8,2,1792]{2,1,0:T(2,128)(2,1)}), bf16[8,2,1792]{2,1,0:T(2,128)(2,1)S(1)}, u32[]{:S(2)}, u32[]{:S(2)}) %all-to-all-start.9) | async-done | bytes 57376 | tf_op jit(solution)/shard_map/all_to_all | solution.py:72
  (59 shorter events, 38.3 us)
Async XLA Ops:
  7.2 97.7 %copy-start = (bf16[1,896,768]{2,1,0:T(8,128)(2,1)S(1)}, bf16[1,896,768]{2,1,0:T(8,128)(2,1)}, u32[]{:S(2)}) copy-start(bf16[1,896,768]{2,1,0:T(8,128)(2,1)} %param.13) | copy-start | bytes 4128772
  8.5 13.0 %all-to-all-start = ((bf16[8,1,1,4]{0,2,1,3:T(2,128)(2,1)}), bf16[8,1,1,4]{0,2,1,3:T(2,128)(2,1)S(1)}, u32[]{:S(2)}, u32[]{:S(2)}) async-start(bf16[8,1,1,4]{0,2,1,3:T(2,128)(2,1)} %broadcast_in_dim.31), calls=%async_computation | async-start | bytes 4096 | tf_op jit(solution)/shard_map/all_to_all | solution.py:62
  22.2 28.7 %all-to-all-start.1 = ((bf16[8,4,1,1]{1,3,2,0:T(2,128)(2,1)}), bf16[8,4,1,1]{1,3,2,0:T(2,128)(2,1)S(1)}, u32[]{:S(2)}, u32[]{:S(2)}) async-start(bf16[8,4,1,1]{1,3,2,0:T(2,128)(2,1)} %copy.37), calls=%async_computation.1 | async-start | bytes 8192 | tf_op jit(solution)/shard_map/all_to_all | solution.py:61
  50.9 30.0 %all-to-all-start.4 = ((bf16[4,2,3584]{2,1,0:T(2,128)(2,1)}), bf16[4,2,3584]{2,1,0:T(2,128)(2,1)S(1)}, u32[]{:S(2)}, u32[]{:S(2)}) async-start(bf16[4,2,3584]{2,1,0:T(2,128)(2,1)} %reshape.182), calls=%async_computation.4 | async-start | bytes 114688 | tf_op jit(solution)/shard_map/all_to_all | solution.py:37
  80.9 9.0 %all-to-all-start.2 = ((bf16[4,2,3584]{2,1,0:T(2,128)(2,1)}), bf16[4,2,3584]{2,1,0:T(2,128)(2,1)S(1)}, u32[]{:S(2)}, u32[]{:S(2)}) async-start(bf16[4,2,3584]{2,1,0:T(2,128)(2,1)} %reshape.184), calls=%async_computation.2 | async-start | bytes 114688 | tf_op jit(solution)/shard_map/all_to_all | solution.py:55
  89.9 11.0 %all-to-all-start.5 = ((bf16[8,4,1,896]{3,1,2,0:T(4,128)(2,1)}), bf16[8,4,1,896]{3,1,2,0:T(4,128)(2,1)S(1)}, u32[]{:S(2)}, u32[]{:S(2)}) async-start(bf16[8,4,1,896]{3,1,2,0:T(4,128)(2,1)} %bitcast.14), calls=%async_computation.5 | async-start | bytes 114688 | tf_op jit(solution)/shard_map/all_to_all | solution.py:36
  99.0 6.7 %copy-start.1 = (bf16[1,896,768]{2,1,0:T(8,128)(2,1)S(1)}, bf16[1,896,768]{2,1,0:T(8,128)(2,1)}, u32[]{:S(2)}) copy-start(bf16[1,896,768]{2,1,0:T(8,128)(2,1)} %param.14) | copy-start | bytes 4128772
  100.9 9.8 %all-to-all-start.3 = ((bf16[8,4,1,896]{3,1,2,0:T(4,128)(2,1)}), bf16[8,4,1,896]{3,1,2,0:T(4,128)(2,1)S(1)}, u32[]{:S(2)}, u32[]{:S(2)}) async-start(bf16[8,4,1,896]{3,1,2,0:T(4,128)(2,1)} %bitcast.8), calls=%async_computation.3 | async-start | bytes 114688 | tf_op jit(solution)/shard_map/all_to_all | solution.py:54
  104.8 51.4 %all-reduce.4.cloned.1.call-start = ((), (), s32[]{:S(2)}) async-start(), calls=%async_computation.10 | async-start | bytes 589824 | tf_op jit(solution)/shard_map/psum | solution.py:44
  105.8 7.4 %copy-start.3 = (u32[32]{0:T(128)S(1)}, u32[32]{0:T(128)}, u32[]{:S(2)}) copy-start(u32[32]{0:T(128)} %constant.38) | copy-start | bytes 388
  105.8 8.6 %copy-start.2 = (s32[1,1,8,1]{2,3,1,0:T(1,128)S(1)}, s32[1,1,8,1]{2,3,1,0:T(1,128)}, u32[]{:S(2)}) copy-start(s32[1,1,8,1]{2,3,1,0:T(1,128)} %param.11) | copy-start | bytes 100
  175.1 8.1 %all-to-all-start.6 = ((bf16[1,4,8,896]{3,2,0,1:T(8,128)(2,1)}), bf16[1,4,8,896]{3,2,0,1:T(8,128)(2,1)S(1)}, u32[]{:S(2)}, u32[]{:S(2)}) async-start(bf16[1,4,8,896]{3,2,0,1:T(8,128)(2,1)} %fusion.27), calls=%async_computation.6 | async-start | bytes 114688 | tf_op jit(solution)/shard_map/all_to_all | solution.py:105
  183.2 8.2 %all-to-all-start.8 = ((bf16[1,4,8,896]{3,2,0,1:T(8,128)(2,1)}), bf16[1,4,8,896]{3,2,0,1:T(8,128)(2,1)S(1)}, u32[]{:S(2)}, u32[]{:S(2)}) async-start(bf16[1,4,8,896]{3,2,0,1:T(8,128)(2,1)} %fusion.24), calls=%async_computation.8 | async-start | bytes 114688 | tf_op jit(solution)/shard_map/all_to_all | solution.py:73
  191.3 10.5 %all-to-all-start.7 = ((bf16[8,2,1792]{2,1,0:T(2,128)(2,1)}), bf16[8,2,1792]{2,1,0:T(2,128)(2,1)S(1)}, u32[]{:S(2)}, u32[]{:S(2)}) async-start(bf16[8,2,1792]{2,1,0:T(2,128)(2,1)} %reshape.186), calls=%async_computation.7 | async-start | bytes 114688 | tf_op jit(solution)/shard_map/all_to_all | solution.py:104
  201.8 9.2 %all-to-all-start.9 = ((bf16[8,2,1792]{2,1,0:T(2,128)(2,1)}), bf16[8,2,1792]{2,1,0:T(2,128)(2,1)S(1)}, u32[]{:S(2)}, u32[]{:S(2)}) async-start(bf16[8,2,1792]{2,1,0:T(2,128)(2,1)} %reshape.188), calls=%async_computation.9 | async-start | bytes 114688 | tf_op jit(solution)/shard_map/all_to_all | solution.py:72
Sparse Core Ops, SparseCore 0:
  113.3 42.8 all-reduce.3
where the time goes:
time: 220 us; the launch traced here: 219 us
  waiting for transfers between devices  55.1 us (25%)
  other arithmetic  49.4 us (22%)
  starting transfers between devices  42 us (19%)
  local copies, waits for them, and re-layouts  28.4 us (13%)
  blocking collectives  15.5 us (7%)
  between operations  14.9 us (7%)
  matrix products  13.3 us (6%)
    unnamed x4, other arithmetic  43.2 us
    psum x1, waiting for transfers between devices, local(): lax.psum((jnp.dot(x_rows, wg, preferred_element_type=jnp.float32), jnp.do...  41.6 us
    unnamed x19, local copies, waits for them, and re-layouts  12.6 us
    all_gather x1, blocking collectives, local(): lax.all_gather(gate_share, 'dp', axis=0, tiled=True)  8.19 us
    all_gather x1, blocking collectives, local(): lax.all_gather(up_share, 'dp', axis=0, tiled=True)  7.34 us
    all_to_all x1, starting transfers between devices, local(): lax.all_to_all(gate_cols, 'dp', split_axis=3, concat_axis=1, tiled=True)  5.16 us
    all_to_all x1, starting transfers between devices, local(): lax.all_to_all(lax.all_to_all(picked_x, 'dp', split_axis=3, concat_axis=1...  5.1 us
    dot_general x3, matrix products, contract_first(): lax.dot_general(left, right, (((0,), (0,)), ((), ())), preferred_element_...  4.91 us
  transfers between devices with their start and end apart: 11, of which 8 were waited for; matrix products, arithmetic and copies ran while one was open for 37% of the time, Pallas kernels for 0%

commit v1 on v0

v1 whole, which is shorter than its diff:
```python
import functools

import jax
import jax.numpy as jnp
from jax import lax
from jax.experimental import pallas as pl
from jax.experimental.pallas import tpu as pltpu
from jax.sharding import PartitionSpec as P

LANES = 128
F32 = jnp.float32
BF16 = jnp.bfloat16
AXES = ("dp", "expert")


def dot(left, right, left_dim=1, right_dim=0):
    return lax.dot_general(
        left, right, (((left_dim,), (right_dim,)), ((), ())), preferred_element_type=F32
    )


def call(body, outs, scratch=()):
    return pl.pallas_call(
        body,
        out_shape=[jax.ShapeDtypeStruct(shape, kind) for shape, kind in outs],
        scratch_shapes=[pltpu.VMEM(shape, kind) for shape, kind in scratch],
        compiler_params=pltpu.CompilerParams(vmem_limit_bytes=40 << 20),
    )


def pick_matrix(route, tokens):
    places = lax.broadcasted_iota(jnp.int32, (route.shape[0], tokens), 1)
    return (places == route).astype(F32).astype(BF16)


def pack_kernel(n_dp, lines, depth, route, gates, tokens, grad_out, message, scratch):
    experts = route.shape[0]
    chunks = tokens.shape[1] // LANES // n_dp
    pick = pick_matrix(route[...], tokens.shape[0])
    scratch[...] = jnp.zeros_like(scratch)
    for source, first in ((tokens, 0), (grad_out, chunks)):
        rows = dot(pick, source[...])
        for i in range(n_dp):
            for k in range(chunks):
                lane = (i * chunks + k) * LANES
                start = i * experts * depth + first + k
                scratch[pl.ds(start, experts, stride=depth), :] = rows[:, lane:lane + LANES]
    gate = jnp.broadcast_to(gates[...].astype(F32), (experts, LANES))
    for i in range(n_dp):
        scratch[pl.ds(i * experts * depth + 2 * chunks, experts, stride=depth), :] = gate
    message[...] = scratch[...].astype(BF16).reshape(message.shape)


def partial_kernel(depth, message, wg, wu, wd, part, x_rows, weighted, gate_col, scratch):
    rows = message.shape[0]
    hidden = wg.shape[1]
    chunks = wg.shape[0] // LANES
    scratch[...] = message[...].astype(F32).reshape(scratch.shape)
    gate = scratch[pl.ds(2 * chunks, rows, stride=depth), :]
    gate_col[...] = gate
    xs, dys = [], []
    for k in range(chunks):
        xs.append(scratch[pl.ds(k, rows, stride=depth), :].astype(BF16))
        dy = scratch[pl.ds(chunks + k, rows, stride=depth), :]
        dys.append(dy.astype(BF16))
        weighted[:, k * LANES:(k + 1) * LANES] = (gate * dy).astype(BF16)
    x = jnp.concatenate(xs, axis=1)
    dy = jnp.concatenate(dys, axis=1)
    x_rows[...] = x
    part[:, :hidden] = dot(x, wg[...]).astype(BF16)
    part[:, hidden:2 * hidden] = dot(x, wu[...]).astype(BF16)
    part[:, 2 * hidden:] = dot(dy, wd[...], 1, 1).astype(BF16)


def middle_kernel(depth, mine, other, gate_col, wg, wu, back, hidden_out, ggp_out, gup_out, scratch):
    rows = mine.shape[0]
    hidden = wg.shape[1]
    chunks = wg.shape[0] // LANES
    pre = mine[...].astype(F32) + other[...].astype(F32)
    gate_pre = pre[:, :hidden]
    up_pre = pre[:, hidden:2 * hidden]
    grad_plain = pre[:, 2 * hidden:]
    sig = 1.0 / (1.0 + jnp.exp(-gate_pre))
    silu = gate_pre * sig
    act = (silu * up_pre).astype(BF16)
    grad = grad_plain * gate_col[:, :1]
    ggp = (grad * up_pre * sig * (1.0 + gate_pre * (1.0 - sig))).astype(BF16)
    gup = (grad * silu).astype(BF16)
    hidden_out[...] = act
    ggp_out[...] = ggp
    gup_out[...] = gup
    result = dot(ggp, wg[...], 1, 1) + dot(gup, wu[...], 1, 1)
    for k in range(chunks):
        scratch[pl.ds(k, rows, stride=depth), :] = result[:, k * LANES:(k + 1) * LANES]
    value = jnp.sum(act.astype(F32) * grad_plain, axis=1, keepdims=True)
    high = value.astype(BF16).astype(F32)
    mid = (value - high).astype(BF16).astype(F32)
    low = value - high - mid
    lane = lax.broadcasted_iota(jnp.int32, (rows, LANES), 1)
    pieces = jnp.where(lane == 0, high, jnp.where(lane == 1, mid, jnp.where(lane == 2, low, 0.0)))
    for k in range(chunks, depth):
        scratch[pl.ds(k, rows, stride=depth), :] = pieces
    back[...] = scratch[...].astype(BF16).reshape(back.shape)


def weights_kernel(x_rows, weighted, act, ggp, gup, grad_wg, grad_wu, grad_wd):
    grad_wg[0] = dot(x_rows[...], ggp[...], 0, 0).astype(BF16)
    grad_wu[0] = dot(x_rows[...], gup[...], 0, 0).astype(BF16)
    grad_wd[0] = dot(act[...], weighted[...], 0, 0).astype(BF16)


def unpack_kernel(n_dp, depth, chunks, route, back, grad_tokens, grad_gates, scratch):
    experts = route.shape[0]
    scratch[...] = back[...].astype(F32).reshape(scratch.shape)
    pick = pick_matrix(route[...], grad_tokens.shape[0])
    for i in range(n_dp):
        first = i * experts * depth
        rows = [
            scratch[pl.ds(first + k, experts, stride=depth), :].astype(BF16)
            for k in range(chunks)
        ]
        lane = i * chunks * LANES
        grad_tokens[:, lane:lane + chunks * LANES] = dot(
            pick, jnp.concatenate(rows, axis=1), 0, 0
        ).astype(BF16)
    pieces = scratch[pl.ds(chunks, experts, stride=depth), :]
    grad_gates[...] = jnp.broadcast_to(
        jnp.sum(pieces, axis=1, keepdims=True), grad_gates.shape
    )


def sum_over_dp(part):
    n_dp = lax.axis_size("dp")
    n_ex = lax.axis_size("expert")
    bits = n_dp.bit_length() - 1
    mine = part
    other = None
    for step in range(bits):
        if other is not None:
            mine = (mine.astype(F32) + other.astype(F32)).astype(BF16)
        pairs = []
        for i in range(n_dp):
            for e in range(n_ex):
                partner = i ^ (1 << ((step + e) % bits))
                pairs.append((i * n_ex + e, partner * n_ex + e))
        other = lax.ppermute(mine, AXES, pairs)
    return mine, other


def local_tiled(tokens, grad_out, route, gates, w_gate, w_up, w_down):
    n_dp = lax.axis_size("dp")
    n_ex = lax.axis_size("expert")
    experts = route.shape[2]
    n_tok, width = tokens.shape
    piece = width // n_dp
    hidden = w_gate.shape[2]
    chunks = piece // LANES
    devices = n_dp * n_ex
    depth = -(-(2 * chunks + 1) // 16) * 16
    back_depth = -(-(chunks + 1) // 8) * 8
    wg, wu, wd = w_gate[0], w_up[0], w_down[0]
    picks = route.reshape(experts, 1)
    gate_in = gates.reshape(experts, 1)

    (message,) = call(
        functools.partial(pack_kernel, n_dp, chunks, depth),
        [((devices, depth, LANES), BF16)],
        [((devices * depth, LANES), F32)],
    )(picks, gate_in, tokens, grad_out)
    arrived = lax.all_to_all(message, AXES, 0, 0, tiled=True)
    part, x_rows, weighted, gate_col = call(
        functools.partial(partial_kernel, depth),
        [
            ((devices, 3 * hidden), BF16),
            ((devices, piece), BF16),
            ((devices, piece), BF16),
            ((devices, LANES), F32),
        ],
        [((devices * depth, LANES), F32)],
    )(arrived, wg, wu, wd)
    mine, other = sum_over_dp(part)
    back, act, ggp, gup = call(
        functools.partial(middle_kernel, back_depth),
        [
            ((devices, back_depth, LANES), BF16),
            ((devices, hidden), BF16),
            ((devices, hidden), BF16),
            ((devices, hidden), BF16),
        ],
        [((devices * back_depth, LANES), F32)],
    )(mine, other, gate_col, wg, wu)
    returned = lax.all_to_all(back, AXES, 0, 0, tiled=True)
    grad_wg, grad_wu, grad_wd = call(
        weights_kernel,
        [(w_gate.shape, BF16), (w_up.shape, BF16), (w_down.shape, BF16)],
    )(x_rows, weighted, act, ggp, gup)
    grad_tokens, grad_gates = call(
        functools.partial(unpack_kernel, n_dp, back_depth, chunks),
        [((n_tok, width), BF16), ((experts, LANES), F32)],
        [((devices * back_depth, LANES), F32)],
    )(picks, returned)
    return grad_tokens, grad_wg, grad_wu, grad_wd, grad_gates[:, 0].reshape(gates.shape)


def local_plain(tokens, grad_out, route, gates, w_gate, w_up, w_down):
    n_dp = lax.axis_size("dp")
    n_ex = lax.axis_size("expert")
    experts, slots = route.shape[2:]
    n_tok, width = tokens.shape
    piece = width // n_dp
    hidden = w_gate.shape[2]
    rows = n_dp * n_ex * slots
    wg, wu, wd = w_gate[0], w_up[0], w_down[0]
    picks = route.reshape(experts * slots)

    def runs(source):
        picked = jnp.take(source, picks, axis=0).reshape(experts, slots, n_dp, piece)
        return picked.transpose(2, 0, 1, 3).reshape(n_dp * experts, slots, piece)

    gate_cols = jnp.broadcast_to(
        gates.reshape(1, experts, slots, 1), (n_dp, experts, slots, 1)
    ).reshape(n_dp * experts, slots, 1)
    message = jnp.concatenate([runs(tokens), runs(grad_out), gate_cols], axis=2)
    arrived = lax.all_to_all(message, AXES, 0, 0, tiled=True).reshape(rows, 2 * piece + 1)
    x_rows, dy_rows = arrived[:, :piece], arrived[:, piece:2 * piece]
    gate = arrived[:, 2 * piece:].astype(F32)
    weighted = (gate * dy_rows.astype(F32)).astype(BF16)
    part = jnp.concatenate(
        [dot(x_rows, wg), dot(x_rows, wu), dot(dy_rows, wd, 1, 1)], axis=1
    )
    pre = lax.psum(part, "dp")
    gate_pre, up_pre, grad_plain = jnp.split(pre, 3, axis=1)
    sig = jax.nn.sigmoid(gate_pre)
    silu = gate_pre * sig
    act = (silu * up_pre).astype(BF16)
    grad = grad_plain * gate
    ggp = (grad * up_pre * sig * (1.0 + gate_pre * (1.0 - sig))).astype(BF16)
    gup = (grad * silu).astype(BF16)
    result = (dot(ggp, wg, 1, 1) + dot(gup, wu, 1, 1)).astype(BF16)
    value = jnp.sum(act.astype(F32) * grad_plain, axis=1, keepdims=True)
    high = value.astype(BF16)
    low = (value - high.astype(F32)).astype(BF16)
    back = jnp.concatenate([result, high, low], axis=1).reshape(n_dp * n_ex, slots, piece + 2)
    returned = lax.all_to_all(back, AXES, 0, 0, tiled=True)
    returned = returned.reshape(n_dp, experts * slots, piece + 2)
    flat = returned[:, :, :piece].transpose(1, 0, 2).reshape(experts * slots, width)
    grad_tokens = jnp.zeros((n_tok, width), F32).at[picks].add(flat.astype(F32)).astype(BF16)
    grad_gates = returned[0, :, piece:].astype(F32).sum(axis=1).reshape(gates.shape)
    return (
        grad_tokens,
        dot(x_rows, ggp, 0, 0).astype(BF16)[None],
        dot(x_rows, gup, 0, 0).astype(BF16)[None],
        dot(act, weighted, 0, 0).astype(BF16)[None],
        grad_gates,
    )


def solution(mesh):
    def local(tokens, grad_out, route, gates, w_gate, w_up, w_down):
        n_dp = lax.axis_size("dp")
        tiled = (
            w_gate.shape[1] % LANES == 0
            and route.shape[2] % 8 == 0
            and route.shape[3] == 1
            and n_dp & (n_dp - 1) == 0
            and n_dp > 1
        )
        body = local_tiled if tiled else local_plain
        return body(tokens, grad_out, route, gates, w_gate, w_up, w_down)

    return jax.shard_map(
        local,
        mesh=mesh,
        in_specs=(
            P(("dp", "expert"), None),
            P(("dp", "expert"), None),
            P("dp", "expert", None, None),
            P("dp", "expert", None, None),
            P("expert", "dp", None),
            P("expert", "dp", None),
            P("expert", None, "dp"),
        ),
        out_specs=(
            P(("dp", "expert"), None),
            P("expert", "dp", None),
            P("expert", "dp", None),
            P("expert", None, "dp"),
            P("dp", "expert", None, None),
        ),
        check_vma=False,
    )
```

time: 220 us -> 48.2 us (0.22)
  other arithmetic: 49.4 us -> 0.04 us
  waiting for transfers between devices: 55.1 us -> 13.4 us
  starting transfers between devices: 42 us -> 4.31 us
  local copies, waits for them, and re-layouts: 28.4 us -> 7.24 us
  between operations: 14.9 us -> 0.67 us
  matrix products: 13.3 us -> 0 us
  Pallas kernels: 0 us -> 6.86 us
    unnamed x4 -> x0, other arithmetic: 43.2 us -> none
    psum x1 -> x0, waiting for transfers between devices: 41.6 us -> none  [local(): lax.psum((jnp.dot(x_rows, wg, preferred_element_type=jnp.float32), jnp.do...]
    all_to_all x10 -> x1, starting transfers between devices: 42 us -> 2.57 us  [local_tiled(): returned = lax.all_to_all(back, AXES, 0, 0, tiled=True)]
    all_gather x2 -> x0, blocking collectives: 15.5 us -> none  [the longest x1 8.19 us: local(): lax.all_gather(gate_share, 'dp', axis=0, tiled=True)]
    all_to_all x0 -> x1, blocking collectives: none -> 15.3 us  [local_tiled(): arrived = lax.all_to_all(message, AXES, 0, 0, tiled=True)]
    dot_general x9 -> x0, matrix products: 13.3 us -> none  [the longest x3 4.91 us: contract_first(): lax.dot_general(left, right, (((0,), (0,)), ((), ())), preferred_element_...]
    all_to_all x10 -> x1, waiting for transfers between devices: 13.4 us -> 4.79 us  [local_tiled(): returned = lax.all_to_all(back, AXES, 0, 0, tiled=True)]
    ppermute x0 -> x2, waiting for transfers between devices: none -> 8.63 us  [sum_over_dp(): other = lax.ppermute(mine, AXES, pairs)]
  transfers between devices with their start and end apart: 11 -> 3, of which waited for: 8 -> 3; matrix products, arithmetic and copies ran while one was open for 37% -> 0% of each run, Pallas kernels for 0% -> 5%
where the time goes in v1:
time: 48.2 us; the launch traced here: 47.8 us
  blocking collectives  15.3 us (32%)
  waiting for transfers between devices  13.4 us (28%)
  local copies, waits for them, and re-layouts  7.24 us (15%)
  Pallas kernels  6.86 us (14%)
  starting transfers between devices  4.31 us (9%)
  between operations  0.67 us (1%)
    all_to_all x1, blocking collectives, local_tiled(): arrived = lax.all_to_all(message, AXES, 0, 0, tiled=True)  15.3 us
    ppermute x2, waiting for transfers between devices, sum_over_dp(): other = lax.ppermute(mine, AXES, pairs)  8.63 us
    unnamed x10, local copies, waits for them, and re-layouts  5.04 us
    all_to_all x1, waiting for transfers between devices, local_tiled(): returned = lax.all_to_all(back, AXES, 0, 0, tiled=True)  4.79 us
    pallas_call x1, Pallas kernels, local_tiled(): call(weights_kernel, [(w_gate.shape, BF16), (w_up.shape, BF16), (w_down.s...  2.6 us
    all_to_all x1, starting transfers between devices, local_tiled(): returned = lax.all_to_all(back, AXES, 0, 0, tiled=True)  2.57 us
    ppermute x2, starting transfers between devices, sum_over_dp(): other = lax.ppermute(mine, AXES, pairs)  1.74 us
    pallas_call x1, Pallas kernels, local_tiled(): call(functools.partial(middle_kernel, back_depth), [((devices, back_depth...  1.58 us
  transfers between devices with their start and end apart: 3, of which 3 were waited for; matrix products, arithmetic and copies ran while one was open for 0% of the time, Pallas kernels for 5%

profile of v1, /device:TPU:0, one launch (start us, length us, event | category | flops | bytes accessed | tf_op | source)
XLA Modules:
  0.0 47.8 jit_solution(15099380050959899020)
XLA Ops:
  0.6 0.0 copy-start
  0.6 0.8 %copy.17.route = s32[8,1]{1,0:T(8,128)S(1)} copy(s32[8,1]{0,1:T(1,128)} %bitcast.11) | data formatting | bytes 64 | tf_op jit(solution)/shard_map/reshape | solution.py:162
  1.5 0.7 %copy.16.gates = bf16[8,1]{1,0:T(8,128)(2,1)S(1)} copy(bf16[8,1]{0,1:T(2,128)(2,1)} %bitcast.12) | data formatting | bytes 32 | tf_op jit(solution)/shard_map/reshape | solution.py:163
  2.2 0.0 copy-start.3
  2.2 1.2 %copy-done.3 = bf16[128,3584]{1,0:T(8,128)(2,1)S(1)} copy-done((bf16[128,3584]{1,0:T(8,128)(2,1)S(1)}, bf16[128,3584]{1,0:T(8,128)(2,1)}, u32[]{:S(2)}) %copy-start.3) | copy-done | bytes 917528
  3.4 0.0 copy-start.4
  3.4 1.2 %copy-done.4 = bf16[128,3584]{1,0:T(8,128)(2,1)S(1)} copy-done((bf16[128,3584]{1,0:T(8,128)(2,1)S(1)}, bf16[128,3584]{1,0:T(8,128)(2,1)}, u32[]{:S(2)}) %copy-start.4) | copy-done | bytes 917528
  4.6 0.4 shard_map.110
  5.0 15.3 %all_to_all.10.message = bf16[32,16,128]{2,1,0:T(8,128)(2,1)S(1)} all-to-all(bf16[32,16,128]{2,1,0:T(8,128)(2,1)S(1)} %shard_map.110), channel_id=1, replica_groups=mesh['dp'=4,'expert'=8] {'dp','expert'}, dimensions={0} | all-to-all | bytes 262144 | tf_op jit(solution)/shard_map/all_to_all | solution.py:170
  20.3 0.0 copy-done
  20.3 0.0 copy-start.1
  20.3 1.3 %copy-done.1 = bf16[1,896,768]{2,1,0:T(8,128)(2,1)S(1)} copy-done((bf16[1,896,768]{2,1,0:T(8,128)(2,1)S(1)}, bf16[1,896,768]{2,1,0:T(8,128)(2,1)}, u32[]{:S(2)}) %copy-start.1) | copy-done | bytes 1376280
  21.6 1.3 %copy-done.2 = bf16[1,768,896]{2,1,0:T(8,128)(2,1)S(1)} copy-done((bf16[1,768,896]{2,1,0:T(8,128)(2,1)S(1)}, bf16[1,768,896]{2,1,0:T(8,128)(2,1)}, u32[]{:S(2)}) %copy-start.2) | copy-done | bytes 1376280
  23.0 0.9 %shard_map.111 = (bf16[32,2304]{1,0:T(8,128)(2,1)S(1)}, bf16[32,896]{1,0:T(8,128)(2,1)S(1)}, bf16[32,896]{1,0:T(8,128)(2,1)S(1)}, f32[32,128]{1,0:T(8,128)S(1)}) custom-call(bf16[32,16,128]{2,1,0:T(8,128)(2,1)S(1)} %all_to_all.10.message, bf16[896,768]{1,0:T(8,128)(2,1)S(1)} %bitcast.6, bf16[896,768]{1,0:T(8,128)(2,1)S(1)} %bitcast.8, ...), custom_call_target="tpu_custom_call" | custom-call | tf_op jit(solution)/shard_map/pallas_call | solution.py:171
  23.8 0.8 %collective-permute-start = (bf16[32,2304]{1,0:T(8,128)(2,1)S(1)}, bf16[32,2304]{1,0:T(8,128)(2,1)S(1)}, u32[]{:S(2)}, u32[]{:S(2)}) collective-permute-start(bf16[32,2304]{1,0:T(8,128)(2,1)S(1)} %get-tuple-element.18), channel_id=1, source_target_pairs={{0,8},{1,17},{2,10},{3,19},{4,12},{5,21},{6,14},{7,23},{8,0},{9,25... | collective-permute-start | bytes 442376 | tf_op jit(solution)/shard_map/ppermute | solution.py:146
  24.7 4.3 %collective-permute-done = bf16[32,2304]{1,0:T(8,128)(2,1)S(1)} collective-permute-done((bf16[32,2304]{1,0:T(8,128)(2,1)S(1)}, bf16[32,2304]{1,0:T(8,128)(2,1)S(1)}, u32[]{:S(2)}, u32[]{:S(2)}) %collective-permute-start) | collective-permute-done | bytes 147488 | tf_op jit(solution)/shard_map/ppermute | solution.py:146
  29.0 0.9 %collective-permute-start.1 = (bf16[32,2304]{1,0:T(8,128)(2,1)S(1)}, bf16[32,2304]{1,0:T(8,128)(2,1)S(1)}, u32[]{:S(2)}, u32[]{:S(2)}) collective-permute-start(bf16[32,2304]{1,0:T(8,128)(2,1)S(1)} %add_convert_fusion.mine), channel_id=1, source_target_pairs={{0,16},{1,9},{2,18},{3,11},{4,20},{5,13},{6,22},{7,15},{8,24},{9,1... | collective-permute-start | bytes 442376 | tf_op jit(solution)/shard_map/ppermute | solution.py:146
  29.9 4.3 %collective-permute-done.1.other = bf16[32,2304]{1,0:T(8,128)(2,1)S(1)} collective-permute-done((bf16[32,2304]{1,0:T(8,128)(2,1)S(1)}, bf16[32,2304]{1,0:T(8,128)(2,1)S(1)}, u32[]{:S(2)}, u32[]{:S(2)}) %collective-permute-start.1) | collective-permute-done | bytes 147488 | tf_op jit(solution)/shard_map/ppermute | solution.py:146
  34.2 1.6 %shard_map.112 = (bf16[32,8,128]{2,1,0:T(8,128)(2,1)}, bf16[32,768]{1,0:T(8,128)(2,1)S(1)}, bf16[32,768]{1,0:T(8,128)(2,1)S(1)}, bf16[32,768]{1,0:T(8,128)(2,1)S(1)}) custom-call(bf16[32,2304]{1,0:T(8,128)(2,1)S(1)} %add_convert_fusion.mine, bf16[32,2304]{1,0:T(8,128)(2,1)S(1)} %collective-permute-done.1.other, f32[32,128]{1,0:T(8,128)S(1)} %get-tuple-element.19.gate_col, ...), custom_call_target="tpu_custom_call" | custom-call | tf_op jit(solution)/shard_map/pallas_call | solution.py:182
  35.8 2.6 %all-to-all-start.1 = ((bf16[32,8,128]{2,1,0:T(8,128)(2,1)}), bf16[32,8,128]{2,1,0:T(8,128)(2,1)S(1)}, u32[]{:S(2)}, u32[]{:S(2)}) async-start(bf16[32,8,128]{2,1,0:T(8,128)(2,1)} %get-tuple-element.20), calls=%async_computation.1 | async-start | bytes 131072 | tf_op jit(solution)/shard_map/all_to_all | solution.py:192
  38.4 2.6 %shard_map.114 = (bf16[1,896,768]{2,1,0:T(8,128)(2,1)}, bf16[1,896,768]{2,1,0:T(8,128)(2,1)}, bf16[1,768,896]{2,1,0:T(8,128)(2,1)}) custom-call(bf16[32,896]{1,0:T(8,128)(2,1)S(1)} %get-tuple-element.22.x_rows, bf16[32,896]{1,0:T(8,128)(2,1)S(1)} %get-tuple-element.23.weighted, bf16[32,768]{1,0:T(8,128)(2,1)S(1)} %get-tuple-element.24.act, ...), custom_call_target="tpu_custom_call" | custom-call | tf_op jit(solution)/shard_map/pallas_call | solution.py:193
  41.0 4.8 %all-to-all-done.1.back = bf16[32,8,128]{2,1,0:T(8,128)(2,1)S(1)} async-done(((bf16[32,8,128]{2,1,0:T(8,128)(2,1)}), bf16[32,8,128]{2,1,0:T(8,128)(2,1)S(1)}, u32[]{:S(2)}, u32[]{:S(2)}) %all-to-all-start.1) | async-done | bytes 65568 | tf_op jit(solution)/shard_map/all_to_all | solution.py:192
  45.8 1.4 %shard_map.113 = (bf16[128,3584]{1,0:T(8,128)(2,1)}, f32[8,128]{1,0:T(8,128)S(1)}) custom-call(s32[8,1]{1,0:T(8,128)S(1)} %copy.17.route, bf16[32,8,128]{2,1,0:T(8,128)(2,1)S(1)} %all-to-all-done.1.back), custom_call_target="tpu_custom_call" | custom-call | tf_op jit(solution)/shard_map/pallas_call | solution.py:197
  47.2 0.6 %slice_reduce_fusion = f32[8]{0:T(128)} fusion(f32[8,128]{1,0:T(8,128)S(1)} %get-tuple-element.30), kind=kLoop, calls=%fused_computation.1 | loop fusion | bytes 64 | tf_op jit(solution)/shard_map/slice | solution.py:202
  (2 shorter events, 0.0 us)
Async XLA Ops:
  0.6 19.6 %copy-start = (bf16[1,896,768]{2,1,0:T(8,128)(2,1)S(1)}, bf16[1,896,768]{2,1,0:T(8,128)(2,1)}, u32[]{:S(2)}) copy-start(bf16[1,896,768]{2,1,0:T(8,128)(2,1)} %param.11) | copy-start | bytes 4128772
  2.2 1.2 %copy-start.3 = (bf16[128,3584]{1,0:T(8,128)(2,1)S(1)}, bf16[128,3584]{1,0:T(8,128)(2,1)}, u32[]{:S(2)}) copy-start(bf16[128,3584]{1,0:T(8,128)(2,1)} %tokens.1) | copy-start | bytes 2752516
  3.4 1.2 %copy-start.4 = (bf16[128,3584]{1,0:T(8,128)(2,1)S(1)}, bf16[128,3584]{1,0:T(8,128)(2,1)}, u32[]{:S(2)}) copy-start(bf16[128,3584]{1,0:T(8,128)(2,1)} %grad_out.1) | copy-start | bytes 2752516
  20.3 1.3 %copy-start.1 = (bf16[1,896,768]{2,1,0:T(8,128)(2,1)S(1)}, bf16[1,896,768]{2,1,0:T(8,128)(2,1)}, u32[]{:S(2)}) copy-start(bf16[1,896,768]{2,1,0:T(8,128)(2,1)} %param.12) | copy-start | bytes 4128772
  21.6 1.3 %copy-start.2 = (bf16[1,768,896]{2,1,0:T(8,128)(2,1)S(1)}, bf16[1,768,896]{2,1,0:T(8,128)(2,1)}, u32[]{:S(2)}) copy-start(bf16[1,768,896]{2,1,0:T(8,128)(2,1)} %param.13) | copy-start | bytes 4128772
  23.8 5.2 %collective-permute-start = (bf16[32,2304]{1,0:T(8,128)(2,1)S(1)}, bf16[32,2304]{1,0:T(8,128)(2,1)S(1)}, u32[]{:S(2)}, u32[]{:S(2)}) collective-permute-start(bf16[32,2304]{1,0:T(8,128)(2,1)S(1)} %get-tuple-element.18), channel_id=1, source_target_pairs={{0,8},{1,17},{2,10},{3,19},{4,12},{5,21},{6,14},{7,23},{8,0},{9,25... | collective-permute-start | bytes 442376 | tf_op jit(solution)/shard_map/ppermute | solution.py:146
  29.0 5.2 %collective-permute-start.1 = (bf16[32,2304]{1,0:T(8,128)(2,1)S(1)}, bf16[32,2304]{1,0:T(8,128)(2,1)S(1)}, u32[]{:S(2)}, u32[]{:S(2)}) collective-permute-start(bf16[32,2304]{1,0:T(8,128)(2,1)S(1)} %add_convert_fusion.mine), channel_id=1, source_target_pairs={{0,16},{1,9},{2,18},{3,11},{4,20},{5,13},{6,22},{7,15},{8,24},{9,1... | collective-permute-start | bytes 442376 | tf_op jit(solution)/shard_map/ppermute | solution.py:146
  35.8 10.0 %all-to-all-start.1 = ((bf16[32,8,128]{2,1,0:T(8,128)(2,1)}), bf16[32,8,128]{2,1,0:T(8,128)(2,1)S(1)}, u32[]{:S(2)}, u32[]{:S(2)}) async-start(bf16[32,8,128]{2,1,0:T(8,128)(2,1)} %get-tuple-element.20), calls=%async_computation.1 | async-start | bytes 131072 | tf_op jit(solution)/shard_map/all_to_all | solution.py:192

commit v2 on v1

--- a/solution.py
+++ b/solution.py
@@ -19,42 +19,119 @@
     )
 
 
-def call(body, outs, scratch=()):
+def call(body, outs, scratch=(), in_hbm=(), out_hbm=(), inputs=0, copies=0, limit=24):
+    def spec(hbm):
+        return pl.BlockSpec(memory_space=pltpu.HBM if hbm else pltpu.VMEM)
+
+    shapes = [pltpu.VMEM(shape, kind) for shape, kind in scratch]
+    if copies:
+        shapes.append(pltpu.SemaphoreType.DMA((copies,)))
     return pl.pallas_call(
         body,
         out_shape=[jax.ShapeDtypeStruct(shape, kind) for shape, kind in outs],
-        scratch_shapes=[pltpu.VMEM(shape, kind) for shape, kind in scratch],
-        compiler_params=pltpu.CompilerParams(vmem_limit_bytes=40 << 20),
-    )
-
-
-def pick_matrix(route, tokens):
-    places = lax.broadcasted_iota(jnp.int32, (route.shape[0], tokens), 1)
-    return (places == route).astype(F32).astype(BF16)
-
-
-def pack_kernel(n_dp, lines, depth, route, gates, tokens, grad_out, message, scratch):
-    experts = route.shape[0]
-    chunks = tokens.shape[1] // LANES // n_dp
-    pick = pick_matrix(route[...], tokens.shape[0])
-    scratch[...] = jnp.zeros_like(scratch)
-    for source, first in ((tokens, 0), (grad_out, chunks)):
-        rows = dot(pick, source[...])
+        in_specs=[spec(k in in_hbm) for k in range(inputs)],
+        out_specs=[spec(k in out_hbm) for k in range(len(outs))],
+        scratch_shapes=shapes,
+        compiler_params=pltpu.CompilerParams(vmem_limit_bytes=limit << 20),
+    )
+
+
+def in_hbm(array):
+    return pltpu.with_memory_space_constraint(array, pltpu.HBM)
+
+
+DP_ORDERS = {4: (0, 1, 3, 2)}
+EXPERT_ORDERS = {8: (7, 1, 4, 0, 3, 6, 5, 2)}
+
+
+def dp_order(n):
+    return DP_ORDERS.get(n, tuple(range(n)))
+
+
+def expert_order(n):
+    return EXPERT_ORDERS.get(n, tuple(range(n)))
+
+
+def match(order):
+    n = len(order)
+    row = lax.broadcasted_iota(jnp.int32, (n, n), 0)
+    column = lax.broadcasted_iota(jnp.int32, (n, n), 1)
+    wanted = jnp.zeros((n, n), jnp.int32)
+    for k, index in enumerate(order):
+        wanted = jnp.where(row == k, index, wanted)
+    return column == wanted
+
+
+def to_column(row, order):
+    n = row.shape[1]
+    spread = jnp.where(match(order), jnp.broadcast_to(row.astype(F32), (n, n)), 0.0)
+    return jnp.sum(spread, axis=1, keepdims=True)
+
+
+def to_row(column, order):
+    n = column.shape[0]
+    spread = jnp.where(match(order), jnp.broadcast_to(column, (n, n)), 0.0)
+    return jnp.sum(spread, axis=0, keepdims=True)
+
+
+def first_lines(n_dp, experts, depth):
+    return [dp_order(n_dp).index(i) * experts * depth for i in range(n_dp)]
+
+
+def exchange(blocks):
+    n_dp = lax.axis_size("dp")
+    n_ex = lax.axis_size("expert")
+    order = [i * n_ex + e for i in dp_order(n_dp) for e in expert_order(n_ex)]
+    return lax.all_to_all(blocks, AXES, 0, 0, tiled=True, axis_index_groups=[order])
+
+
+def pack_kernel(
+    n_dp, depth, route, gates, tokens, grad_out, w_down, message, wd, picks,
+    held, scratch, route_in, gates_in, sems,
+):
+    experts = route.shape[1]
+    width = tokens.shape[1]
+    piece = width // n_dp
+    chunks = piece // LANES
+    targets = (held.at[0], held.at[1], route_in, gates_in, wd)
+    copies = [
+        pltpu.make_async_copy(source, target, sems.at[s])
+        for s, (source, target) in enumerate(zip((tokens, grad_out, route, gates, w_down), targets))
+    ]
+    for s in (2, 3, 0, 1, 4):
+        copies[s].start()
+    copies[2].wait()
+    copies[3].wait()
+    places = lax.broadcasted_iota(jnp.int32, (experts, tokens.shape[0]), 1).astype(F32)
+    column = to_column(route_in[...], expert_order(experts))
+    picks[...] = (places == column).astype(F32)
+    pick = picks[...].astype(BF16)
+    gate = jnp.broadcast_to(to_column(gates_in[...], expert_order(experts)), (experts, LANES))
+    zero = jnp.zeros((experts, LANES), F32)
+    firsts = first_lines(n_dp, experts, depth)
+    for first in firsts:
+        for k in range(2 * chunks, depth):
+            scratch[pl.ds(first + k, experts, stride=depth), :] = gate if k == 2 * chunks else zero
+    for s in range(2):
+        copies[s].wait()
+        rows = dot(pick, held[s])
         for i in range(n_dp):
             for k in range(chunks):
-                lane = (i * chunks + k) * LANES
-                start = i * experts * depth + first + k
+                start = firsts[i] + s * chunks + k
+                lane = i * piece + k * LANES
                 scratch[pl.ds(start, experts, stride=depth), :] = rows[:, lane:lane + LANES]
-    gate = jnp.broadcast_to(gates[...].astype(F32), (experts, LANES))
-    for i in range(n_dp):
-        scratch[pl.ds(i * experts * depth + 2 * chunks, experts, stride=depth), :] = gate
     message[...] = scratch[...].astype(BF16).reshape(message.shape)
-
-
-def partial_kernel(depth, message, wg, wu, wd, part, x_rows, weighted, gate_col, scratch):
+    copies[4].wait()
+
+
+def partial_kernel(
+    depth, message, wg, w_up, wd, part, x_rows, weighted, gate_col, wu, scratch, sems
+):
     rows = message.shape[0]
-    hidden = wg.shape[1]
-    chunks = wg.shape[0] // LANES
+    _, hidden, piece = wd.shape
+    chunks = piece // LANES
+    copy = pltpu.make_async_copy(w_up, wu, sems.at[0])
+    copy.start()
     scratch[...] = message[...].astype(F32).reshape(scratch.shape)
     gate = scratch[pl.ds(2 * chunks, rows, stride=depth), :]
     gate_col[...] = gate
@@ -67,16 +144,31 @@
     x = jnp.concatenate(xs, axis=1)
     dy = jnp.concatenate(dys, axis=1)
     x_rows[...] = x
-    part[:, :hidden] = dot(x, wg[...]).astype(BF16)
-    part[:, hidden:2 * hidden] = dot(x, wu[...]).astype(BF16)
-    part[:, 2 * hidden:] = dot(dy, wd[...], 1, 1).astype(BF16)
-
-
-def middle_kernel(depth, mine, other, gate_col, wg, wu, back, hidden_out, ggp_out, gup_out, scratch):
-    rows = mine.shape[0]
-    hidden = wg.shape[1]
-    chunks = wg.shape[0] // LANES
-    pre = mine[...].astype(F32) + other[...].astype(F32)
+    part[:, :hidden] = dot(x, wg[0]).astype(BF16)
+    part[:, 2 * hidden:] = dot(dy, wd[0], 1, 1).astype(BF16)
+    copy.wait()
+    part[:, hidden:2 * hidden] = dot(x, wu[0]).astype(BF16)
+
+
+def turn_kernel(wg, wu, turned):
+    hidden = wg.shape[2]
+    for s, source in enumerate((wg, wu)):
+        for k in range(hidden // LANES):
+            first = s * hidden + k * LANES
+            turned[first:first + LANES, :] = source[0, :, k * LANES:(k + 1) * LANES].T
+
+
+def middle_kernel(depth, count, *refs):
+    parts, (gate_col, turned, back, hidden_out, ggp_out, gup_out, scratch) = (
+        refs[:count], refs[count:]
+    )
+    rows = parts[0].shape[0]
+    hidden = turned.shape[0] // 2
+    chunks = turned.shape[1] // LANES
+    terms = [part[...].astype(F32) for part in parts]
+    while len(terms) > 1:
+        terms = [terms[k] + terms[k + 1] for k in range(0, len(terms), 2)]
+    pre = terms[0]
     gate_pre = pre[:, :hidden]
     up_pre = pre[:, hidden:2 * hidden]
     grad_plain = pre[:, 2 * hidden:]
@@ -89,7 +181,7 @@
     hidden_out[...] = act
     ggp_out[...] = ggp
     gup_out[...] = gup
-    result = dot(ggp, wg[...], 1, 1) + dot(gup, wu[...], 1, 1)
+    result = dot(jnp.concatenate([ggp, gup], axis=1), turned[...])
     for k in range(chunks):
         scratch[pl.ds(k, rows, stride=depth), :] = result[:, k * LANES:(k + 1) * LANES]
     value = jnp.sum(act.astype(F32) * grad_plain, axis=1, keepdims=True)
@@ -109,42 +201,34 @@
     grad_wd[0] = dot(act[...], weighted[...], 0, 0).astype(BF16)
 
 
-def unpack_kernel(n_dp, depth, chunks, route, back, grad_tokens, grad_gates, scratch):
-    experts = route.shape[0]
+def unpack_kernel(
+    n_dp, depth, chunks, picks, back, grad_tokens, grad_gates, scratch, held, gates_held, sems
+):
+    experts = picks.shape[0]
+    piece = chunks * LANES
+    firsts = first_lines(n_dp, experts, depth)
     scratch[...] = back[...].astype(F32).reshape(scratch.shape)
-    pick = pick_matrix(route[...], grad_tokens.shape[0])
+    pick = picks[...].astype(BF16)
+    column = jnp.sum(scratch[pl.ds(firsts[0] + chunks, experts, stride=depth), :], axis=1, keepdims=True)
+    gates_held[...] = to_row(column, expert_order(experts))
+    copies = [pltpu.make_async_copy(gates_held, grad_gates, sems.at[n_dp])]
+    copies[0].start()
     for i in range(n_dp):
-        first = i * experts * depth
+        first = firsts[i]
         rows = [
             scratch[pl.ds(first + k, experts, stride=depth), :].astype(BF16)
             for k in range(chunks)
         ]
-        lane = i * chunks * LANES
-        grad_tokens[:, lane:lane + chunks * LANES] = dot(
+        lanes = pl.ds(i * piece, piece)
+        held[:, i * piece:(i + 1) * piece] = dot(
             pick, jnp.concatenate(rows, axis=1), 0, 0
         ).astype(BF16)
-    pieces = scratch[pl.ds(chunks, experts, stride=depth), :]
-    grad_gates[...] = jnp.broadcast_to(
-        jnp.sum(pieces, axis=1, keepdims=True), grad_gates.shape
-    )
-
-
-def sum_over_dp(part):
-    n_dp = lax.axis_size("dp")
-    n_ex = lax.axis_size("expert")
-    bits = n_dp.bit_length() - 1
-    mine = part
-    other = None
-    for step in range(bits):
-        if other is not None:
-            mine = (mine.astype(F32) + other.astype(F32)).astype(BF16)
-        pairs = []
-        for i in range(n_dp):
-            for e in range(n_ex):
-                partner = i ^ (1 << ((step + e) % bits))
-                pairs.append((i * n_ex + e, partner * n_ex + e))
-        other = lax.ppermute(mine, AXES, pairs)
-    return mine, other
+        copies.append(
+            pltpu.make_async_copy(held.at[:, lanes], grad_tokens.at[:, lanes], sems.at[i])
+        )
+        copies[-1].start()
+    for copy in copies:
+        copy.wait()
 
 
 def local_tiled(tokens, grad_out, route, gates, w_gate, w_up, w_down):
@@ -158,29 +242,44 @@
     devices = n_dp * n_ex
     depth = -(-(2 * chunks + 1) // 16) * 16
     back_depth = -(-(chunks + 1) // 8) * 8
-    wg, wu, wd = w_gate[0], w_up[0], w_down[0]
-    picks = route.reshape(experts, 1)
-    gate_in = gates.reshape(experts, 1)
-
-    (message,) = call(
-        functools.partial(pack_kernel, n_dp, chunks, depth),
-        [((devices, depth, LANES), BF16)],
-        [((devices * depth, LANES), F32)],
-    )(picks, gate_in, tokens, grad_out)
-    arrived = lax.all_to_all(message, AXES, 0, 0, tiled=True)
-    part, x_rows, weighted, gate_col = call(
+    picks = route.reshape(1, experts)
+    gate_in = gates.reshape(1, experts)
+
+    message, wd, chosen = call(
+        functools.partial(pack_kernel, n_dp, depth),
+        [((devices, depth, LANES), BF16), (w_down.shape, BF16), ((experts, n_tok), F32)],
+        [
+            ((2, n_tok, width), BF16),
+            ((devices * depth, LANES), F32),
+            ((1, experts), jnp.int32),
+            ((1, experts), BF16),
+        ],
+        in_hbm=(0, 1, 2, 3, 4),
+        inputs=5,
+        copies=5,
+    )(*map(in_hbm, (picks, gate_in, tokens, grad_out, w_down)))
+    arrived = exchange(message)
+    part, x_rows, weighted, gate_col, wu = call(
         functools.partial(partial_kernel, depth),
         [
             ((devices, 3 * hidden), BF16),
             ((devices, piece), BF16),
             ((devices, piece), BF16),
             ((devices, LANES), F32),
+            ((1, piece, hidden), BF16),
         ],
         [((devices * depth, LANES), F32)],
-    )(arrived, wg, wu, wd)
-    mine, other = sum_over_dp(part)
+        in_hbm=(2,),
+        inputs=4,
+        copies=1,
+    )(arrived, w_gate, in_hbm(w_up), wd)
+    parts = {0: part}
+    for k in sorted(range(1, n_dp), key=lambda k: (k & -k, k), reverse=True):
+        parts[k] = lax.ppermute(part, "dp", [(i, i ^ k) for i in range(n_dp)])
+    parts = [parts[k] for k in range(n_dp)]
+    (turned,) = call(turn_kernel, [((2 * hidden, piece), BF16)], inputs=2)(w_gate, wu)
     back, act, ggp, gup = call(
-        functools.partial(middle_kernel, back_depth),
+        functools.partial(middle_kernel, back_depth, n_dp),
         [
             ((devices, back_depth, LANES), BF16),
             ((devices, hidden), BF16),
@@ -188,18 +287,27 @@
             ((devices, hidden), BF16),
         ],
         [((devices * back_depth, LANES), F32)],
-    )(mine, other, gate_col, wg, wu)
-    returned = lax.all_to_all(back, AXES, 0, 0, tiled=True)
+        inputs=n_dp + 2,
+    )(*parts, gate_col, turned)
+    returned = exchange(back)
     grad_wg, grad_wu, grad_wd = call(
         weights_kernel,
         [(w_gate.shape, BF16), (w_up.shape, BF16), (w_down.shape, BF16)],
+        inputs=5,
     )(x_rows, weighted, act, ggp, gup)
     grad_tokens, grad_gates = call(
         functools.partial(unpack_kernel, n_dp, back_depth, chunks),
-        [((n_tok, width), BF16), ((experts, LANES), F32)],
-        [((devices * back_depth, LANES), F32)],
-    )(picks, returned)
-    return grad_tokens, grad_wg, grad_wu, grad_wd, grad_gates[:, 0].reshape(gates.shape)
+        [((n_tok, width), BF16), ((1, experts), F32)],
+        [
+            ((devices * back_depth, LANES), F32),
+            ((n_tok, width), BF16),
+            ((1, experts), F32),
+        ],
+        out_hbm=(0, 1),
+        inputs=2,
+        copies=n_dp + 1,
+    )(chosen, returned)
+    return grad_tokens, grad_wg, grad_wu, grad_wd, grad_gates.reshape(gates.shape)
 
 
 def local_plain(tokens, grad_out, route, gates, w_gate, w_up, w_down):
@@ -261,9 +369,10 @@
         tiled = (
             w_gate.shape[1] % LANES == 0
             and route.shape[2] % 8 == 0
+            and route.shape[2] == lax.axis_size("expert")
             and route.shape[3] == 1
+            and w_gate.shape[2] % LANES == 0
             and n_dp & (n_dp - 1) == 0
-            and n_dp > 1
         )
         body = local_tiled if tiled else local_plain
         return body(tokens, grad_out, route, gates, w_gate, w_up, w_down)

time: 48.2 us -> 41.3 us (0.86)
  local copies, waits for them, and re-layouts: 7.24 us -> 0.01 us
  waiting for transfers between devices: 13.4 us -> 10.2 us
  Pallas kernels: 6.86 us -> 9.59 us
  starting transfers between devices: 4.31 us -> 6.12 us
  blocking collectives: 15.3 us -> 14.5 us
    unnamed x10 -> x2, local copies, waits for them, and re-layouts: 5.04 us -> 0.01 us
    ppermute x2 -> x3, waiting for transfers between devices: 8.63 us -> 5.56 us  [local_tiled(): parts[k] = lax.ppermute(part, 'dp', [(i, i ^ k) for i in range(n_dp)])]
    pallas_call x2 -> x3, Pallas kernels: 1.98 us -> 4.03 us  [the longest x1 2.07 us: local_tiled(): call(functools.partial(pack_kernel, n_dp, depth), [((devices, depth, LANE...]
    ppermute x2 -> x3, starting transfers between devices: 1.74 us -> 3.55 us  [local_tiled(): parts[k] = lax.ppermute(part, 'dp', [(i, i ^ k) for i in range(n_dp)])]
    reshape x2 -> x0, local copies, waits for them, and re-layouts: 1.58 us -> none  [the longest x1 0.84 us: local_tiled(): picks = route.reshape(experts, 1)]
    pallas_call x1, Pallas kernels: 0.87 us -> 1.74 us  [local_tiled(): call(functools.partial(partial_kernel, depth), [((devices, 3 * hidden), B...]
    all_to_all x1, blocking collectives: 15.3 us -> 14.5 us  [exchange(): lax.all_to_all(blocks, AXES, 0, 0, tiled=True, axis_index_groups=[order])]
    slice x1 -> x0, local copies, waits for them, and re-layouts: 0.62 us -> none  [local_tiled(): grad_gates[:, 0].reshape(gates.shape)]
  transfers between devices with their start and end apart: 3 -> 4, of which waited for: 3 -> 3; matrix products, arithmetic and copies ran while one was open for 0% -> 0% of each run, Pallas kernels for 5% -> 8%
where the time goes in v2:
time: 41.3 us; the launch traced here: 41 us
  blocking collectives  14.5 us (35%)
  waiting for transfers between devices  10.2 us (25%)
  Pallas kernels  9.59 us (23%)
  starting transfers between devices  6.12 us (15%)
  between operations  0.68 us (2%)
    all_to_all x1, blocking collectives, exchange(): lax.all_to_all(blocks, AXES, 0, 0, tiled=True, axis_index_groups=[order])  14.5 us
    ppermute x3, waiting for transfers between devices, local_tiled(): parts[k] = lax.ppermute(part, 'dp', [(i, i ^ k) for i in range(n_dp)])  5.56 us
    all_to_all x1, waiting for transfers between devices, exchange(): lax.all_to_all(blocks, AXES, 0, 0, tiled=True, axis_index_groups=[order])  4.59 us
    ppermute x3, starting transfers between devices, local_tiled(): parts[k] = lax.ppermute(part, 'dp', [(i, i ^ k) for i in range(n_dp)])  3.55 us
    pallas_call x1, Pallas kernels, local_tiled(): call(weights_kernel, [(w_gate.shape, BF16), (w_up.shape, BF16), (w_down.s...  2.6 us
    all_to_all x1, starting transfers between devices, exchange(): lax.all_to_all(blocks, AXES, 0, 0, tiled=True, axis_index_groups=[order])  2.57 us
    pallas_call x1, Pallas kernels, local_tiled(): call(functools.partial(pack_kernel, n_dp, depth), [((devices, depth, LANE...  2.07 us
    pallas_call x1, Pallas kernels, local_tiled(): call(functools.partial(partial_kernel, depth), [((devices, 3 * hidden), B...  1.74 us
  transfers between devices with their start and end apart: 4, of which 3 were waited for; matrix products, arithmetic and copies ran while one was open for 0% of the time, Pallas kernels for 8%

profile of v2, /device:TPU:0, one launch (start us, length us, event | category | flops | bytes accessed | tf_op | source)
XLA Modules:
  0.0 41.0 jit_solution(3400897166321688683)
XLA Ops:
  0.6 0.0 copy-start
  0.6 2.1 %shard_map.110 = (bf16[32,16,128]{2,1,0:T(8,128)(2,1)S(1)}, bf16[1,768,896]{2,1,0:T(8,128)(2,1)S(1)}, f32[8,128]{1,0:T(8,128)S(1)}) custom-call(s32[1,8]{1,0:T(1,128)} %bitcast.3, bf16[1,8]{1,0:T(2,128)(2,1)} %bitcast.4, bf16[128,3584]{1,0:T(8,128)(2,1)} %tokens.1, bf16[128,3584]{1,0:T(8,128)(2,1)} %grad_out.1, bf16[1,768,896]{2,1,0:T(8,128)(2,1)} %w_down.1), custom_call_target="tpu_custom_call" | custom-call | tf_op jit(solution)/shard_map/pallas_call | solution.py:248
  2.7 14.5 %all_to_all.10.message = bf16[32,16,128]{2,1,0:T(8,128)(2,1)S(1)} all-to-all(bf16[32,16,128]{2,1,0:T(8,128)(2,1)S(1)} %get-tuple-element.23), channel_id=1, replica_groups={{7,1,4,0,3,6,5,2,15,9,12,8,11,14,13,10,31,25,28,24,27,30,29,26,23,17,20..., dimensions={0} | all-to-all | bytes 262144 | tf_op jit(solution)/shard_map/all_to_all | solution.py:85
  17.2 0.0 copy-done
  17.2 1.7 %shard_map.111 = (bf16[32,2304]{1,0:T(8,128)(2,1)S(1)}, bf16[32,896]{1,0:T(8,128)(2,1)S(1)}, bf16[32,896]{1,0:T(8,128)(2,1)S(1)}, f32[32,128]{1,0:T(8,128)S(1)}, bf16[1,896,768]{2,1,0:T(8,128)(2,1)S(1)}) custom-call(bf16[32,16,128]{2,1,0:T(8,128)(2,1)S(1)} %all_to_all.10.message, bf16[1,896,768]{2,1,0:T(8,128)(2,1)S(1)} %copy-done, ...), custom_call_target="tpu_custom_call" | custom-call | tf_op jit(solution)/shard_map/pallas_call | solution.py:262
  19.0 0.8 %collective-permute-start = (bf16[32,2304]{1,0:T(8,128)(2,1)S(1)}, bf16[32,2304]{1,0:T(8,128)(2,1)S(1)}, u32[]{:S(2)}, u32[]{:S(2)}) collective-permute-start(bf16[32,2304]{1,0:T(8,128)(2,1)S(1)} %get-tuple-element.25.refs_0_), channel_id=1, source_target_pairs={{0,8},{8,0},{16,24},{24,16},{1,9},{9,1},{17,25},{25,17},{2,10},{10... | collective-permute-start | bytes 442376 | tf_op jit(solution)/shard_map/ppermute | solution.py:278
  19.8 1.2 %collective-permute-start.1 = (bf16[32,2304]{1,0:T(8,128)(2,1)S(1)}, bf16[32,2304]{1,0:T(8,128)(2,1)S(1)}, u32[]{:S(2)}, u32[]{:S(2)}) collective-permute-start(bf16[32,2304]{1,0:T(8,128)(2,1)S(1)} %get-tuple-element.25.refs_0_), channel_id=1, source_target_pairs={{0,16},{8,24},{16,0},{24,8},{1,17},{9,25},{17,1},{25,9},{2,18},{10... | collective-permute-start | bytes 442376 | tf_op jit(solution)/shard_map/ppermute | solution.py:278
  21.0 1.6 %collective-permute-start.2 = (bf16[32,2304]{1,0:T(8,128)(2,1)S(1)}, bf16[32,2304]{1,0:T(8,128)(2,1)S(1)}, u32[]{:S(2)}, u32[]{:S(2)}) collective-permute-start(bf16[32,2304]{1,0:T(8,128)(2,1)S(1)} %get-tuple-element.25.refs_0_), channel_id=1, source_target_pairs={{0,24},{8,16},{16,8},{24,0},{1,25},{9,17},{17,9},{25,1},{2,26},{10... | collective-permute-start | bytes 442376 | tf_op jit(solution)/shard_map/ppermute | solution.py:278
  22.5 0.8 %shard_map.112.refs_5_ = bf16[1536,896]{1,0:T(8,128)(2,1)S(1)} custom-call(bf16[1,896,768]{2,1,0:T(8,128)(2,1)S(1)} %copy-done, bf16[1,896,768]{2,1,0:T(8,128)(2,1)S(1)} %get-tuple-element.27.wu), custom_call_target="tpu_custom_call" | custom-call | tf_op jit(solution)/shard_map/pallas_call | solution.py:280
  23.3 2.4 %collective-permute-done.refs_1_ = bf16[32,2304]{1,0:T(8,128)(2,1)S(1)} collective-permute-done((bf16[32,2304]{1,0:T(8,128)(2,1)S(1)}, bf16[32,2304]{1,0:T(8,128)(2,1)S(1)}, u32[]{:S(2)}, u32[]{:S(2)}) %collective-permute-start) | collective-permute-done | bytes 147488 | tf_op jit(solution)/shard_map/ppermute | solution.py:278
  25.7 3.1 %collective-permute-done.1.refs_2_ = bf16[32,2304]{1,0:T(8,128)(2,1)S(1)} collective-permute-done((bf16[32,2304]{1,0:T(8,128)(2,1)S(1)}, bf16[32,2304]{1,0:T(8,128)(2,1)S(1)}, u32[]{:S(2)}, u32[]{:S(2)}) %collective-permute-start.1) | collective-permute-done | bytes 147488 | tf_op jit(solution)/shard_map/ppermute | solution.py:278
  28.9 0.0 collective-permute-done.2.refs_3_
  28.9 1.2 %shard_map.113 = (bf16[32,8,128]{2,1,0:T(8,128)(2,1)}, bf16[32,768]{1,0:T(8,128)(2,1)S(1)}, bf16[32,768]{1,0:T(8,128)(2,1)S(1)}, bf16[32,768]{1,0:T(8,128)(2,1)S(1)}) custom-call(bf16[32,2304]{1,0:T(8,128)(2,1)S(1)} %get-tuple-element.25.refs_0_, bf16[32,2304]{1,0:T(8,128)(2,1)S(1)} %collective-permute-done.refs_1_, ...), custom_call_target="tpu_custom_call" | custom-call | tf_op jit(solution)/shard_map/pallas_call | solution.py:281
  30.1 2.6 %all-to-all-start.1 = ((bf16[32,8,128]{2,1,0:T(8,128)(2,1)}), bf16[32,8,128]{2,1,0:T(8,128)(2,1)S(1)}, u32[]{:S(2)}, u32[]{:S(2)}) async-start(bf16[32,8,128]{2,1,0:T(8,128)(2,1)} %get-tuple-element.28), calls=%async_computation.1 | async-start | bytes 131072 | tf_op jit(solution)/shard_map/all_to_all | solution.py:85
  32.6 2.6 %shard_map.115 = (bf16[1,896,768]{2,1,0:T(8,128)(2,1)}, bf16[1,896,768]{2,1,0:T(8,128)(2,1)}, bf16[1,768,896]{2,1,0:T(8,128)(2,1)}) custom-call(bf16[32,896]{1,0:T(8,128)(2,1)S(1)} %get-tuple-element.30.x_rows, bf16[32,896]{1,0:T(8,128)(2,1)S(1)} %get-tuple-element.31.weighted, bf16[32,768]{1,0:T(8,128)(2,1)S(1)} %get-tuple-element.32.act, ...), custom_call_target="tpu_custom_call" | custom-call | tf_op jit(solution)/shard_map/pallas_call | solution.py:293
  35.2 4.6 %all-to-all-done.1.back = bf16[32,8,128]{2,1,0:T(8,128)(2,1)S(1)} async-done(((bf16[32,8,128]{2,1,0:T(8,128)(2,1)}), bf16[32,8,128]{2,1,0:T(8,128)(2,1)S(1)}, u32[]{:S(2)}, u32[]{:S(2)}) %all-to-all-start.1) | async-done | bytes 65568 | tf_op jit(solution)/shard_map/all_to_all | solution.py:85
  39.8 1.2 %shard_map.114 = (bf16[128,3584]{1,0:T(8,128)(2,1)}, f32[1,8]{1,0:T(1,128)}) custom-call(f32[8,128]{1,0:T(8,128)S(1)} %get-tuple-element.22.picks, bf16[32,8,128]{2,1,0:T(8,128)(2,1)S(1)} %all-to-all-done.1.back), custom_call_target="tpu_custom_call" | custom-call | tf_op jit(solution)/shard_map/pallas_call | solution.py:298
Async XLA Ops:
  0.6 16.6 %copy-start = (bf16[1,896,768]{2,1,0:T(8,128)(2,1)S(1)}, bf16[1,896,768]{2,1,0:T(8,128)(2,1)}, u32[]{:S(2)}) copy-start(bf16[1,896,768]{2,1,0:T(8,128)(2,1)} %wg.3) | copy-start | bytes 4128772
  19.0 6.7 %collective-permute-start = (bf16[32,2304]{1,0:T(8,128)(2,1)S(1)}, bf16[32,2304]{1,0:T(8,128)(2,1)S(1)}, u32[]{:S(2)}, u32[]{:S(2)}) collective-permute-start(bf16[32,2304]{1,0:T(8,128)(2,1)S(1)} %get-tuple-element.25.refs_0_), channel_id=1, source_target_pairs={{0,8},{8,0},{16,24},{24,16},{1,9},{9,1},{17,25},{25,17},{2,10},{10... | collective-permute-start | bytes 442376 | tf_op jit(solution)/shard_map/ppermute | solution.py:278
  19.8 9.1 %collective-permute-start.1 = (bf16[32,2304]{1,0:T(8,128)(2,1)S(1)}, bf16[32,2304]{1,0:T(8,128)(2,1)S(1)}, u32[]{:S(2)}, u32[]{:S(2)}) collective-permute-start(bf16[32,2304]{1,0:T(8,128)(2,1)S(1)} %get-tuple-element.25.refs_0_), channel_id=1, source_target_pairs={{0,16},{8,24},{16,0},{24,8},{1,17},{9,25},{17,1},{25,9},{2,18},{10... | collective-permute-start | bytes 442376 | tf_op jit(solution)/shard_map/ppermute | solution.py:278
  21.0 7.9 %collective-permute-start.2 = (bf16[32,2304]{1,0:T(8,128)(2,1)S(1)}, bf16[32,2304]{1,0:T(8,128)(2,1)S(1)}, u32[]{:S(2)}, u32[]{:S(2)}) collective-permute-start(bf16[32,2304]{1,0:T(8,128)(2,1)S(1)} %get-tuple-element.25.refs_0_), channel_id=1, source_target_pairs={{0,24},{8,16},{16,8},{24,0},{1,25},{9,17},{17,9},{25,1},{2,26},{10... | collective-permute-start | bytes 442376 | tf_op jit(solution)/shard_map/ppermute | solution.py:278
  30.1 9.8 %all-to-all-start.1 = ((bf16[32,8,128]{2,1,0:T(8,128)(2,1)}), bf16[32,8,128]{2,1,0:T(8,128)(2,1)S(1)}, u32[]{:S(2)}, u32[]{:S(2)}) async-start(bf16[32,8,128]{2,1,0:T(8,128)(2,1)} %get-tuple-element.28), calls=%async_computation.1 | async-start | bytes 131072 | tf_op jit(solution)/shard_map/all_to_all | solution.py:85

commit v3 on v2

--- a/solution.py
+++ b/solution.py
@@ -19,7 +19,7 @@
     )
 
 
-def call(body, outs, scratch=(), in_hbm=(), out_hbm=(), inputs=0, copies=0, limit=24):
+def call(body, outs, scratch=(), in_hbm=(), out_hbm=(), inputs=0, copies=0, limit=24, cost=None):
     def spec(hbm):
         return pl.BlockSpec(memory_space=pltpu.HBM if hbm else pltpu.VMEM)
 
@@ -32,6 +32,7 @@
         in_specs=[spec(k in in_hbm) for k in range(inputs)],
         out_specs=[spec(k in out_hbm) for k in range(len(outs))],
         scratch_shapes=shapes,
+        cost_estimate=cost,
         compiler_params=pltpu.CompilerParams(vmem_limit_bytes=limit << 20),
     )
 
@@ -124,14 +125,10 @@
     copies[4].wait()
 
 
-def partial_kernel(
-    depth, message, wg, w_up, wd, part, x_rows, weighted, gate_col, wu, scratch, sems
-):
+def partial_kernel(depth, message, wg, wd, part, x_rows, weighted, gate_col, scratch):
     rows = message.shape[0]
     _, hidden, piece = wd.shape
     chunks = piece // LANES
-    copy = pltpu.make_async_copy(w_up, wu, sems.at[0])
-    copy.start()
     scratch[...] = message[...].astype(F32).reshape(scratch.shape)
     gate = scratch[pl.ds(2 * chunks, rows, stride=depth), :]
     gate_col[...] = gate
@@ -145,9 +142,11 @@
     dy = jnp.concatenate(dys, axis=1)
     x_rows[...] = x
     part[:, :hidden] = dot(x, wg[0]).astype(BF16)
-    part[:, 2 * hidden:] = dot(dy, wd[0], 1, 1).astype(BF16)
-    copy.wait()
-    part[:, hidden:2 * hidden] = dot(x, wu[0]).astype(BF16)
+    part[:, hidden:] = dot(dy, wd[0], 1, 1).astype(BF16)
+
+
+def up_kernel(x_rows, wu, part):
+    part[...] = dot(x_rows[...], wu[0]).astype(BF16)
 
 
 def turn_kernel(wg, wu, turned):
@@ -158,20 +157,23 @@
             turned[first:first + LANES, :] = source[0, :, k * LANES:(k + 1) * LANES].T
 
 
-def middle_kernel(depth, count, *refs):
-    parts, (gate_col, turned, back, hidden_out, ggp_out, gup_out, scratch) = (
-        refs[:count], refs[count:]
-    )
-    rows = parts[0].shape[0]
+def sum_kernel(*refs):
+    terms = [ref[...].astype(F32) for ref in refs[:-1]]
+    while len(terms) > 1:
+        terms = [terms[k] + terms[k + 1] for k in range(0, len(terms), 2)]
+    refs[-1][...] = terms[0]
+
+
+def middle_kernel(
+    depth, up, mine, other, gate_col, turned, back, hidden_out, ggp_out, gup_out, scratch
+):
+    rows = gate_col.shape[0]
     hidden = turned.shape[0] // 2
     chunks = turned.shape[1] // LANES
-    terms = [part[...].astype(F32) for part in parts]
-    while len(terms) > 1:
-        terms = [terms[k] + terms[k + 1] for k in range(0, len(terms), 2)]
-    pre = terms[0]
-    gate_pre = pre[:, :hidden]
-    up_pre = pre[:, hidden:2 * hidden]
-    grad_plain = pre[:, 2 * hidden:]
+    up_pre = up[...]
+    rest = mine[...].astype(F32) + other[...].astype(F32)
+    gate_pre = rest[:, :hidden]
+    grad_plain = rest[:, hidden:]
     sig = 1.0 / (1.0 + jnp.exp(-gate_pre))
     silu = gate_pre * sig
     act = (silu * up_pre).astype(BF16)
@@ -231,6 +233,35 @@
         copy.wait()
 
 
+def dp_terms(paired, direct):
+    n_dp = lax.axis_size("dp")
+    n_ex = lax.axis_size("expert")
+    bits = n_dp.bit_length() - 1
+
+    def swap(array, masks):
+        return lax.ppermute(
+            array,
+            AXES,
+            [
+                (i * n_ex + e, (i ^ masks[e % 2]) * n_ex + e)
+                for i in range(n_dp)
+                for e in range(n_ex)
+            ],
+        )
+
+    def mask(step, core):
+        return 1 << ((step + core) % bits)
+
+    other = swap(paired, (mask(0, 0), mask(0, 1)))
+    masks = [(mask(k, 0), mask(k, 1)) for k in range(bits)]
+    masks += [(k, k) for k in range(1, n_dp) if k & (k - 1)]
+    direct_all = [direct] + [swap(direct, pair) for pair in masks]
+    for step in range(1, bits):
+        paired = (paired.astype(F32) + other.astype(F32)).astype(BF16)
+        other = swap(paired, (mask(step, 0), mask(step, 1)))
+    return (paired, other), direct_all
+
+
 def local_tiled(tokens, grad_out, route, gates, w_gate, w_up, w_down):
     n_dp = lax.axis_size("dp")
     n_ex = lax.axis_size("expert")
@@ -259,27 +290,33 @@
         copies=5,
     )(*map(in_hbm, (picks, gate_in, tokens, grad_out, w_down)))
     arrived = exchange(message)
-    part, x_rows, weighted, gate_col, wu = call(
+    part, x_rows, weighted, gate_col = call(
         functools.partial(partial_kernel, depth),
         [
-            ((devices, 3 * hidden), BF16),
+            ((devices, 2 * hidden), BF16),
             ((devices, piece), BF16),
             ((devices, piece), BF16),
             ((devices, LANES), F32),
-            ((1, piece, hidden), BF16),
         ],
         [((devices * depth, LANES), F32)],
-        in_hbm=(2,),
-        inputs=4,
-        copies=1,
-    )(arrived, w_gate, in_hbm(w_up), wd)
-    parts = {0: part}
-    for k in sorted(range(1, n_dp), key=lambda k: (k & -k, k), reverse=True):
-        parts[k] = lax.ppermute(part, "dp", [(i, i ^ k) for i in range(n_dp)])
-    parts = [parts[k] for k in range(n_dp)]
-    (turned,) = call(turn_kernel, [((2 * hidden, piece), BF16)], inputs=2)(w_gate, wu)
+        inputs=3,
+    )(arrived, w_gate, wd)
+    (up_part,) = call(
+        up_kernel,
+        [((devices, hidden), BF16)],
+        inputs=2,
+        cost=pl.CostEstimate(flops=3 * 10**8, bytes_accessed=0, transcendentals=0),
+    )(x_rows, w_up)
+    (mine, other), direct = dp_terms(part, up_part)
+    (up_pre,) = call(
+        sum_kernel,
+        [((devices, hidden), F32)],
+        inputs=n_dp,
+        cost=pl.CostEstimate(flops=10**9, bytes_accessed=0, transcendentals=0),
+    )(*direct)
+    (turned,) = call(turn_kernel, [((2 * hidden, piece), BF16)], inputs=2)(w_gate, w_up)
     back, act, ggp, gup = call(
-        functools.partial(middle_kernel, back_depth, n_dp),
+        functools.partial(middle_kernel, back_depth),
         [
             ((devices, back_depth, LANES), BF16),
             ((devices, hidden), BF16),
@@ -287,8 +324,8 @@
             ((devices, hidden), BF16),
         ],
         [((devices * back_depth, LANES), F32)],
-        inputs=n_dp + 2,
-    )(*parts, gate_col, turned)
+        inputs=5,
+    )(up_pre, mine, other, gate_col, turned)
     returned = exchange(back)
     grad_wg, grad_wu, grad_wd = call(
         weights_kernel,

time: 41.3 us -> 40.4 us (0.978)
  waiting for transfers between devices: 10.2 us -> 7.32 us
  starting transfers between devices: 6.12 us -> 8.69 us
  Pallas kernels: 9.59 us -> 8.91 us
    ppermute x3 -> x5, waiting for transfers between devices: 5.56 us -> 2.73 us  [swap(): lax.ppermute(array, AXES, [(i * n_ex + e, (i ^ masks[e % 2]) * n_ex + e)...]
    ppermute x3 -> x5, starting transfers between devices: 3.55 us -> 5.61 us  [swap(): lax.ppermute(array, AXES, [(i * n_ex + e, (i ^ masks[e % 2]) * n_ex + e)...]
    pallas_call x3 -> x5, Pallas kernels: 3.7 us -> 3.03 us  [the longest x1 1.26 us: local_tiled(): call(functools.partial(middle_kernel, back_depth), [((devices, back_depth...]
    all_to_all x1, starting transfers between devices: 2.57 us -> 3.09 us  [exchange(): lax.all_to_all(blocks, AXES, 0, 0, tiled=True, axis_index_groups=[order])]
  transfers between devices with their start and end apart: 4 -> 6, of which waited for: 3 -> 4; matrix products, arithmetic and copies ran while one was open for 0% -> 0% of each run, Pallas kernels for 8% -> 9%
where the time goes in v3:
time: 40.4 us; the launch traced here: 40.1 us
  blocking collectives  14.5 us (36%)
  Pallas kernels  8.91 us (22%)
  starting transfers between devices  8.69 us (22%)
  waiting for transfers between devices  7.32 us (18%)
  between operations  0.7 us (2%)
    all_to_all x1, blocking collectives, exchange(): lax.all_to_all(blocks, AXES, 0, 0, tiled=True, axis_index_groups=[order])  14.5 us
    ppermute x5, starting transfers between devices, swap(): lax.ppermute(array, AXES, [(i * n_ex + e, (i ^ masks[e % 2]) * n_ex + e)...  5.61 us
    all_to_all x1, waiting for transfers between devices, exchange(): lax.all_to_all(blocks, AXES, 0, 0, tiled=True, axis_index_groups=[order])  4.59 us
    all_to_all x1, starting transfers between devices, exchange(): lax.all_to_all(blocks, AXES, 0, 0, tiled=True, axis_index_groups=[order])  3.09 us
    ppermute x5, waiting for transfers between devices, swap(): lax.ppermute(array, AXES, [(i * n_ex + e, (i ^ masks[e % 2]) * n_ex + e)...  2.73 us
    pallas_call x1, Pallas kernels, local_tiled(): call(weights_kernel, [(w_gate.shape, BF16), (w_up.shape, BF16), (w_down.s...  2.6 us
    pallas_call x1, Pallas kernels, local_tiled(): call(functools.partial(pack_kernel, n_dp, depth), [((devices, depth, LANE...  2.07 us
    pallas_call x1, Pallas kernels, local_tiled(): call(functools.partial(middle_kernel, back_depth), [((devices, back_depth...  1.26 us
  transfers between devices with their start and end apart: 6, of which 4 were waited for; matrix products, arithmetic and copies ran while one was open for 0% of the time, Pallas kernels for 9%

profile of v3, /device:TPU:0, one launch (start us, length us, event | category | flops | bytes accessed | tf_op | source)
XLA Modules:
  0.0 40.1 jit_solution(17038457108623025835)
XLA Ops:
  0.6 0.0 copy-start
  0.6 2.1 %shard_map.110 = (bf16[32,16,128]{2,1,0:T(8,128)(2,1)S(1)}, bf16[1,768,896]{2,1,0:T(8,128)(2,1)S(1)}, f32[8,128]{1,0:T(8,128)S(1)}) custom-call(s32[1,8]{1,0:T(1,128)} %bitcast.3, bf16[1,8]{1,0:T(2,128)(2,1)} %bitcast.4, bf16[128,3584]{1,0:T(8,128)(2,1)} %tokens.1, bf16[128,3584]{1,0:T(8,128)(2,1)} %grad_out.1, bf16[1,768,896]{2,1,0:T(8,128)(2,1)} %w_down.1), custom_call_target="tpu_custom_call" | custom-call | tf_op jit(solution)/shard_map/pallas_call | solution.py:279
  2.7 14.5 %all_to_all.10.message = bf16[32,16,128]{2,1,0:T(8,128)(2,1)S(1)} all-to-all(bf16[32,16,128]{2,1,0:T(8,128)(2,1)S(1)} %get-tuple-element.22), channel_id=1, replica_groups={{7,1,4,0,3,6,5,2,15,9,12,8,11,14,13,10,31,25,28,24,27,30,29,26,23,17,20..., dimensions={0} | all-to-all | bytes 262144 | tf_op jit(solution)/shard_map/all_to_all | solution.py:86
  17.2 0.0 copy-done
  17.2 0.0 copy-start.1
  17.2 0.7 %shard_map.111 = (bf16[32,1536]{1,0:T(8,128)(2,1)S(1)}, bf16[32,896]{1,0:T(8,128)(2,1)S(1)}, bf16[32,896]{1,0:T(8,128)(2,1)S(1)}, f32[32,128]{1,0:T(8,128)S(1)}) custom-call(bf16[32,16,128]{2,1,0:T(8,128)(2,1)S(1)} %all_to_all.10.message, bf16[1,896,768]{2,1,0:T(8,128)(2,1)S(1)} %copy-done, bf16[1,768,896]{2,1,0:T(8,128)(2,1)S(1)} %get-tuple-element.23.wd), custom_call_target="tpu_custom_call" | custom-call | tf_op jit(solution)/shard_map/pallas_call | solution.py:293
  17.9 0.8 %collective-permute-start.3 = (bf16[32,1536]{1,0:T(8,128)(2,1)S(1)}, bf16[32,1536]{1,0:T(8,128)(2,1)S(1)}, u32[]{:S(2)}, u32[]{:S(2)}) collective-permute-start(bf16[32,1536]{1,0:T(8,128)(2,1)S(1)} %get-tuple-element.25), channel_id=1, source_target_pairs={{0,8},{1,17},{2,10},{3,19},{4,12},{5,21},{6,14},{7,23},{8,0},{9,25... | collective-permute-start | bytes 294920 | tf_op jit(solution)/shard_map/ppermute | solution.py:242
  18.7 0.0 copy-done.1
  18.7 0.3 shard_map.112.refs_0_
  19.0 1.4 %collective-permute-start = (bf16[32,768]{1,0:T(8,128)(2,1)S(1)}, bf16[32,768]{1,0:T(8,128)(2,1)S(1)}, u32[]{:S(2)}, u32[]{:S(2)}) collective-permute-start(bf16[32,768]{1,0:T(8,128)(2,1)S(1)} %shard_map.112.refs_0_), channel_id=1, source_target_pairs={{0,8},{1,17},{2,10},{3,19},{4,12},{5,21},{6,14},{7,23},{8,0},{9,25... | collective-permute-start | bytes 147464 | tf_op jit(solution)/shard_map/ppermute | solution.py:242
  20.4 0.5 %collective-permute-start.1 = (bf16[32,768]{1,0:T(8,128)(2,1)S(1)}, bf16[32,768]{1,0:T(8,128)(2,1)S(1)}, u32[]{:S(2)}, u32[]{:S(2)}) collective-permute-start(bf16[32,768]{1,0:T(8,128)(2,1)S(1)} %shard_map.112.refs_0_), channel_id=1, source_target_pairs={{0,16},{1,9},{2,18},{3,11},{4,20},{5,13},{6,22},{7,15},{8,24},{9,1... | collective-permute-start | bytes 147464 | tf_op jit(solution)/shard_map/ppermute | solution.py:242
  20.9 1.7 %collective-permute-start.2 = (bf16[32,768]{1,0:T(8,128)(2,1)S(1)}, bf16[32,768]{1,0:T(8,128)(2,1)S(1)}, u32[]{:S(2)}, u32[]{:S(2)}) collective-permute-start(bf16[32,768]{1,0:T(8,128)(2,1)S(1)} %shard_map.112.refs_0_), channel_id=1, source_target_pairs={{0,24},{1,25},{2,26},{3,27},{4,28},{5,29},{6,30},{7,31},{8,16},{9,... | collective-permute-start | bytes 147464 | tf_op jit(solution)/shard_map/ppermute | solution.py:242
  22.6 0.0 collective-permute-done.3
  22.6 1.3 %collective-permute-start.4 = (bf16[32,1536]{1,0:T(8,128)(2,1)S(1)}, bf16[32,1536]{1,0:T(8,128)(2,1)S(1)}, u32[]{:S(2)}, u32[]{:S(2)}) collective-permute-start(bf16[32,1536]{1,0:T(8,128)(2,1)S(1)} %add_convert_fusion.mine), channel_id=1, source_target_pairs={{0,16},{1,9},{2,18},{3,11},{4,20},{5,13},{6,22},{7,15},{8,24},{9,1... | collective-permute-start | bytes 294920 | tf_op jit(solution)/shard_map/ppermute | solution.py:242
  23.9 0.8 %shard_map.114.turned = bf16[1536,896]{1,0:T(8,128)(2,1)S(1)} custom-call(bf16[1,896,768]{2,1,0:T(8,128)(2,1)S(1)} %copy-done, bf16[1,896,768]{2,1,0:T(8,128)(2,1)S(1)} %copy-done.1), custom_call_target="tpu_custom_call" | custom-call | tf_op jit(solution)/shard_map/pallas_call | solution.py:317
  24.6 0.0 collective-permute-done.refs_1_
  24.6 0.3 collective-permute-done.1.refs_2_
  25.0 1.4 %collective-permute-done.2.refs_3_ = bf16[32,768]{1,0:T(8,128)(2,1)S(1)} collective-permute-done((bf16[32,768]{1,0:T(8,128)(2,1)S(1)}, bf16[32,768]{1,0:T(8,128)(2,1)S(1)}, u32[]{:S(2)}, u32[]{:S(2)}) %collective-permute-start.2) | collective-permute-done | bytes 49184 | tf_op jit(solution)/shard_map/ppermute | solution.py:242
  26.5 0.9 %collective-permute-done.4.other = bf16[32,1536]{1,0:T(8,128)(2,1)S(1)} collective-permute-done((bf16[32,1536]{1,0:T(8,128)(2,1)S(1)}, bf16[32,1536]{1,0:T(8,128)(2,1)S(1)}, u32[]{:S(2)}, u32[]{:S(2)}) %collective-permute-start.4) | collective-permute-done | bytes 98336 | tf_op jit(solution)/shard_map/ppermute | solution.py:242
  27.4 1.3 %shard_map.115 = (bf16[32,8,128]{2,1,0:T(8,128)(2,1)}, bf16[32,768]{1,0:T(8,128)(2,1)S(1)}, bf16[32,768]{1,0:T(8,128)(2,1)S(1)}, bf16[32,768]{1,0:T(8,128)(2,1)S(1)}) custom-call(f32[32,768]{1,0:T(8,128)S(1)} %shard_map.113.up, bf16[32,1536]{1,0:T(8,128)(2,1)S(1)} %add_convert_fusion.mine, bf16[32,1536]{1,0:T(8,128)(2,1)S(1)} %collective-permute-done.4.other, ...), custom_call_target="tpu_custom_call" | custom-call | tf_op jit(solution)/shard_map/pallas_call | solution.py:318
  28.7 3.1 %all-to-all-start.1 = ((bf16[32,8,128]{2,1,0:T(8,128)(2,1)}), bf16[32,8,128]{2,1,0:T(8,128)(2,1)S(1)}, u32[]{:S(2)}, u32[]{:S(2)}) async-start(bf16[32,8,128]{2,1,0:T(8,128)(2,1)} %get-tuple-element.27), calls=%async_computation.1 | async-start | bytes 131072 | tf_op jit(solution)/shard_map/all_to_all | solution.py:86
  31.7 2.6 %shard_map.117 = (bf16[1,896,768]{2,1,0:T(8,128)(2,1)}, bf16[1,896,768]{2,1,0:T(8,128)(2,1)}, bf16[1,768,896]{2,1,0:T(8,128)(2,1)}) custom-call(bf16[32,896]{1,0:T(8,128)(2,1)S(1)} %get-tuple-element.24.x_rows, bf16[32,896]{1,0:T(8,128)(2,1)S(1)} %get-tuple-element.29.weighted, bf16[32,768]{1,0:T(8,128)(2,1)S(1)} %get-tuple-element.30.act, ...), custom_call_target="tpu_custom_call" | custom-call | tf_op jit(solution)/shard_map/pallas_call | solution.py:330
  34.3 4.6 %all-to-all-done.1.back = bf16[32,8,128]{2,1,0:T(8,128)(2,1)S(1)} async-done(((bf16[32,8,128]{2,1,0:T(8,128)(2,1)}), bf16[32,8,128]{2,1,0:T(8,128)(2,1)S(1)}, u32[]{:S(2)}, u32[]{:S(2)}) %all-to-all-start.1) | async-done | bytes 65568 | tf_op jit(solution)/shard_map/all_to_all | solution.py:86
  38.9 1.2 %shard_map.116 = (bf16[128,3584]{1,0:T(8,128)(2,1)}, f32[1,8]{1,0:T(1,128)}) custom-call(f32[8,128]{1,0:T(8,128)S(1)} %get-tuple-element.21.picks, bf16[32,8,128]{2,1,0:T(8,128)(2,1)S(1)} %all-to-all-done.1.back), custom_call_target="tpu_custom_call" | custom-call | tf_op jit(solution)/shard_map/pallas_call | solution.py:335
  (2 shorter events, 0.1 us)
Async XLA Ops:
  0.6 16.6 %copy-start = (bf16[1,896,768]{2,1,0:T(8,128)(2,1)S(1)}, bf16[1,896,768]{2,1,0:T(8,128)(2,1)}, u32[]{:S(2)}) copy-start(bf16[1,896,768]{2,1,0:T(8,128)(2,1)} %wg.3) | copy-start | bytes 4128772
  17.2 1.5 %copy-start.1 = (bf16[1,896,768]{2,1,0:T(8,128)(2,1)S(1)}, bf16[1,896,768]{2,1,0:T(8,128)(2,1)}, u32[]{:S(2)}) copy-start(bf16[1,896,768]{2,1,0:T(8,128)(2,1)} %wu.3) | copy-start | bytes 4128772
  17.9 4.7 %collective-permute-start.3 = (bf16[32,1536]{1,0:T(8,128)(2,1)S(1)}, bf16[32,1536]{1,0:T(8,128)(2,1)S(1)}, u32[]{:S(2)}, u32[]{:S(2)}) collective-permute-start(bf16[32,1536]{1,0:T(8,128)(2,1)S(1)} %get-tuple-element.25), channel_id=1, source_target_pairs={{0,8},{1,17},{2,10},{3,19},{4,12},{5,21},{6,14},{7,23},{8,0},{9,25... | collective-permute-start | bytes 294920 | tf_op jit(solution)/shard_map/ppermute | solution.py:242
  19.0 5.6 %collective-permute-start = (bf16[32,768]{1,0:T(8,128)(2,1)S(1)}, bf16[32,768]{1,0:T(8,128)(2,1)S(1)}, u32[]{:S(2)}, u32[]{:S(2)}) collective-permute-start(bf16[32,768]{1,0:T(8,128)(2,1)S(1)} %shard_map.112.refs_0_), channel_id=1, source_target_pairs={{0,8},{1,17},{2,10},{3,19},{4,12},{5,21},{6,14},{7,23},{8,0},{9,25... | collective-permute-start | bytes 147464 | tf_op jit(solution)/shard_map/ppermute | solution.py:242
  20.4 4.6 %collective-permute-start.1 = (bf16[32,768]{1,0:T(8,128)(2,1)S(1)}, bf16[32,768]{1,0:T(8,128)(2,1)S(1)}, u32[]{:S(2)}, u32[]{:S(2)}) collective-permute-start(bf16[32,768]{1,0:T(8,128)(2,1)S(1)} %shard_map.112.refs_0_), channel_id=1, source_target_pairs={{0,16},{1,9},{2,18},{3,11},{4,20},{5,13},{6,22},{7,15},{8,24},{9,1... | collective-permute-start | bytes 147464 | tf_op jit(solution)/shard_map/ppermute | solution.py:242
  20.9 5.5 %collective-permute-start.2 = (bf16[32,768]{1,0:T(8,128)(2,1)S(1)}, bf16[32,768]{1,0:T(8,128)(2,1)S(1)}, u32[]{:S(2)}, u32[]{:S(2)}) collective-permute-start(bf16[32,768]{1,0:T(8,128)(2,1)S(1)} %shard_map.112.refs_0_), channel_id=1, source_target_pairs={{0,24},{1,25},{2,26},{3,27},{4,28},{5,29},{6,30},{7,31},{8,16},{9,... | collective-permute-start | bytes 147464 | tf_op jit(solution)/shard_map/ppermute | solution.py:242
  22.6 4.8 %collective-permute-start.4 = (bf16[32,1536]{1,0:T(8,128)(2,1)S(1)}, bf16[32,1536]{1,0:T(8,128)(2,1)S(1)}, u32[]{:S(2)}, u32[]{:S(2)}) collective-permute-start(bf16[32,1536]{1,0:T(8,128)(2,1)S(1)} %add_convert_fusion.mine), channel_id=1, source_target_pairs={{0,16},{1,9},{2,18},{3,11},{4,20},{5,13},{6,22},{7,15},{8,24},{9,1... | collective-permute-start | bytes 294920 | tf_op jit(solution)/shard_map/ppermute | solution.py:242
  28.7 10.3 %all-to-all-start.1 = ((bf16[32,8,128]{2,1,0:T(8,128)(2,1)}), bf16[32,8,128]{2,1,0:T(8,128)(2,1)S(1)}, u32[]{:S(2)}, u32[]{:S(2)}) async-start(bf16[32,8,128]{2,1,0:T(8,128)(2,1)} %get-tuple-element.27), calls=%async_computation.1 | async-start | bytes 131072 | tf_op jit(solution)/shard_map/all_to_all | solution.py:86
